TPU v7x, 32 devices: a whole 2x2x4 slice. The times are simulated.
32 devices in a mesh: ctx: 8 (over z, x), fsdp: 4 (over y, core).
Axes of the slice: x: 2, y: 2, z: 4, core: 2. Of those that a mesh axis runs over, the one named last changes fastest.
Arguments:
- inputs: bfloat16 [8, 512, 768], P('fsdp', 'ctx'), may hold values from -6 to 6
- w_qkv: bfloat16 [2, 3, 768, 768], P(None, None, ('ctx', 'fsdp')), may hold values from -0.21650635 to 0.21650635
- w_out: bfloat16 [2, 768, 768], P(None, ('ctx', 'fsdp')), may hold values from -4.8989795 to 4.8989795
- w_up: bfloat16 [2, 768, 3072], P(None, ('ctx', 'fsdp')), may hold values from -0.21875 to 0.21875
- w_down: bfloat16 [2, 3072, 768], P(None, ('ctx', 'fsdp')), may hold values from -0.109375 to 0.109375
- biases: bfloat16 [2, 3, 768], P(None, None, ('ctx', 'fsdp')), may hold values from -1.75 to 1.75
- value_bias: bfloat16 [2, 768], P(None, ('ctx', 'fsdp')), may hold values from -0.078125 to 0.078125
- up_bias: bfloat16 [2, 3072], P(None, ('ctx', 'fsdp')), may hold values from -1.75 to 1.75
- gains: bfloat16 [2, 2, 768], P(None, None, ('ctx', 'fsdp')), may hold values from 0.5 to 1.5
- shifts: bfloat16 [2, 2, 768], P(None, None, ('ctx', 'fsdp')), may hold values from -1.75 to 1.75
- cotangent: bfloat16 [8, 512, 768], P('fsdp', 'ctx'), may hold values from -8 to 8
Outputs:
- output: bfloat16 [8, 512, 768], P('fsdp', 'ctx')
- grad_inputs: bfloat16 [8, 512, 768], P('fsdp', 'ctx')
- grad_w_qkv: float32 [2, 3, 768, 768], P(None, None, ('ctx', 'fsdp'))
- grad_w_out: float32 [2, 768, 768], P(None, ('ctx', 'fsdp'))
- grad_w_up: float32 [2, 768, 3072], P(None, ('ctx', 'fsdp'))
- grad_w_down: float32 [2, 3072, 768], P(None, ('ctx', 'fsdp'))
- grad_biases: float32 [2, 3, 768], P(None, None, ('ctx', 'fsdp'))
- grad_value_bias: float32 [2, 768], P(None, ('ctx', 'fsdp'))
- grad_up_bias: float32 [2, 3072], P(None, ('ctx', 'fsdp'))
- grad_gains: float32 [2, 2, 768], P(None, None, ('ctx', 'fsdp'))
- grad_shifts: float32 [2, 2, 768], P(None, None, ('ctx', 'fsdp'))
All inputs are finite; a program needn't handle non-finite values.
Results may differ from a plain program's by a relative error of at most 0.024.
Values may be sent and summed in bfloat16 or wider, within the bound.
A program may use at most 320 MiB of HBM per device.

v0:
```python
import jax
import jax.numpy as jnp
from jax import lax
from jax.sharding import PartitionSpec as P

D = 768
HEADS = 12
HEAD_DIM = 64
LAYERS = 2


def part_count(row_count):
    count = 1
    while row_count % count != 0 or row_count // count > 2048:
        count = count + 1
    return count


def exact_gelu(values):
    return jax.nn.gelu(values, approximate=False)


def normalize(values, gain, shift):
    centred = values - jnp.mean(values, axis=1, keepdims=True)
    inv_std = lax.rsqrt(jnp.mean(centred * centred, axis=1, keepdims=True) + 1e-12)
    scaled = centred * inv_std
    return (scaled * gain + shift, scaled, inv_std)


def norm_back(grad, scaled, inv_std, gain):
    weighted = grad * gain
    return (
        weighted
        - jnp.mean(weighted, axis=1, keepdims=True)
        - scaled * jnp.mean(weighted * scaled, axis=1, keepdims=True)
    ) * inv_std


def split_heads(seq_array, count):
    seq_count, width, unused = seq_array.shape
    return seq_array.reshape(seq_count, count, width // count, HEADS, HEAD_DIM).transpose(
        1, 0, 2, 3, 4
    )


def merge_heads(head_array):
    seq_count, unused, row_count, unused_dim = head_array.shape
    return head_array.transpose(0, 2, 1, 3).reshape(seq_count * row_count, HEADS * HEAD_DIM)


def attend_forward(queries, keys, values):
    seq_count, row_count, unused = queries.shape
    factor = HEAD_DIM ** (-0.5)
    query_heads = queries.reshape(seq_count, row_count, HEADS, HEAD_DIM)
    start_state = (
        jnp.full((seq_count, HEADS, row_count), -1e30, jnp.float32),
        jnp.zeros((seq_count, HEADS, row_count), jnp.float32),
        jnp.zeros((seq_count, HEADS, row_count, HEAD_DIM), jnp.float32),
    )
    piece = (
        lax.all_gather(keys, "ctx", axis=1, tiled=True),
        lax.all_gather(values, "ctx", axis=1, tiled=True),
    )
    count = part_count(piece[0].shape[1])

    def attend_advance(inner, parts):
        peak, totals, accum = inner
        key_part, value_part = parts
        scores = (
            jnp.einsum("sthd,skhd->shtk", query_heads, key_part, preferred_element_type=jnp.float32)
            * factor
        )
        new_peak = jnp.maximum(peak, jnp.max(scores, axis=3))
        decay = jnp.exp(peak - new_peak)
        weights = jnp.exp(scores - new_peak[..., None])
        totals = totals * decay + jnp.sum(weights, axis=3)
        accum = accum * decay[..., None] + jnp.einsum(
            "shtk,skhd->shtd",
            weights.astype(jnp.bfloat16),
            value_part,
            preferred_element_type=jnp.float32,
        )
        return ((new_peak, totals, accum), None)

    result, _ = lax.scan(
        attend_advance, start_state, (split_heads(piece[0], count), split_heads(piece[1], count))
    )
    peak, totals, accum = result
    mixed = merge_heads(accum / totals[..., None])
    return (mixed, peak + jnp.log(totals))


def query_fold(queries, grad_mixed, logsum, row_delta, keys, values):
    seq_count, row_count, unused = queries.shape
    factor = HEAD_DIM ** (-0.5)
    query_heads = queries.reshape(seq_count, row_count, HEADS, HEAD_DIM)
    grad_heads = grad_mixed.reshape(seq_count, row_count, HEADS, HEAD_DIM)
    start_state = jnp.zeros((seq_count, HEADS, row_count, HEAD_DIM), jnp.float32)
    piece = (
        lax.all_gather(keys, "ctx", axis=1, tiled=True),
        lax.all_gather(values, "ctx", axis=1, tiled=True),
    )
    count = part_count(piece[0].shape[1])

    def query_advance(totals, parts):
        key_part, value_part = parts
        scores = (
            jnp.einsum("sthd,skhd->shtk", query_heads, key_part, preferred_element_type=jnp.float32)
            * factor
        )
        weights = jnp.exp(scores - logsum[..., None])
        grad_weights = jnp.einsum(
            "sthd,skhd->shtk", grad_heads, value_part, preferred_element_type=jnp.float32
        )
        grad_scores = (weights * (grad_weights - row_delta[..., None])).astype(jnp.bfloat16)
        return (
            totals
            + jnp.einsum(
                "shtk,skhd->shtd", grad_scores, key_part, preferred_element_type=jnp.float32
            )
            * factor,
            None,
        )

    result, _ = lax.scan(
        query_advance, start_state, (split_heads(piece[0], count), split_heads(piece[1], count))
    )
    return result


def key_fold(queries, grad_mixed, keys, values, all_logsum, all_delta):
    seq_count, row_count, unused = keys.shape
    factor = HEAD_DIM ** (-0.5)
    key_heads = keys.reshape(seq_count, row_count, HEADS, HEAD_DIM)
    value_heads = values.reshape(seq_count, row_count, HEADS, HEAD_DIM)
    start_state = (
        jnp.zeros((seq_count, HEADS, row_count, HEAD_DIM), jnp.float32),
        jnp.zeros((seq_count, HEADS, row_count, HEAD_DIM), jnp.float32),
    )
    piece = (
        lax.all_gather(queries, "ctx", axis=1, tiled=True),
        lax.all_gather(grad_mixed, "ctx", axis=1, tiled=True),
    )
    width = piece[0].shape[1]
    count = part_count(width)
    block = width // count
    log_parts = all_logsum.reshape(seq_count, HEADS, count, block).transpose(2, 0, 1, 3)
    delta_parts = all_delta.reshape(seq_count, HEADS, count, block).transpose(2, 0, 1, 3)

    def key_advance(inner, parts):
        grad_keys, grad_values = inner
        query_part, grad_part, log_part, delta_part = parts
        scores = (
            jnp.einsum("sqhd,skhd->shqk", query_part, key_heads, preferred_element_type=jnp.float32)
            * factor
        )
        weights = jnp.exp(scores - log_part[..., None])
        grad_values = grad_values + jnp.einsum(
            "shqk,sqhd->shkd",
            weights.astype(jnp.bfloat16),
            grad_part,
            preferred_element_type=jnp.float32,
        )
        grad_weights = jnp.einsum(
            "sqhd,skhd->shqk", grad_part, value_heads, preferred_element_type=jnp.float32
        )
        grad_scores = (weights * (grad_weights - delta_part[..., None])).astype(jnp.bfloat16)
        grad_keys = (
            grad_keys
            + jnp.einsum(
                "shqk,sqhd->shkd", grad_scores, query_part, preferred_element_type=jnp.float32
            )
            * factor
        )
        return ((grad_keys, grad_values), None)

    result, _ = lax.scan(
        key_advance,
        start_state,
        (split_heads(piece[0], count), split_heads(piece[1], count), log_parts, delta_parts),
    )
    return result


def forward_layer(stream, full, seq_count):
    w_attn, w_mix, w_raise, w_lower, bias_rows, bias_value, bias_raise, gain_rows, shift_rows = full
    total_rows = stream.shape[0]
    rounded = stream.astype(jnp.bfloat16)
    projected = jnp.einsum("td,cde->cte", rounded, w_attn, preferred_element_type=jnp.float32)
    queries = (projected[0] + bias_rows[0].astype(jnp.float32)).astype(jnp.bfloat16)
    keys = projected[1].astype(jnp.bfloat16)
    values = (projected[2] + bias_value.astype(jnp.float32)).astype(jnp.bfloat16)
    seq_shape = (seq_count, total_rows // seq_count, D)
    mixed, logsum = attend_forward(
        queries.reshape(seq_shape), keys.reshape(seq_shape), values.reshape(seq_shape)
    )
    mixed_low = mixed.astype(jnp.bfloat16)
    branch = jnp.dot(mixed_low, w_mix, preferred_element_type=jnp.float32) + bias_rows[1].astype(
        jnp.float32
    )
    normed, scaled_one, inv_one = normalize(
        stream + branch, gain_rows[0].astype(jnp.float32), shift_rows[0].astype(jnp.float32)
    )
    normed_low = normed.astype(jnp.bfloat16)
    upward = jnp.dot(normed_low, w_raise, preferred_element_type=jnp.float32) + bias_raise.astype(
        jnp.float32
    )
    active = exact_gelu(upward).astype(jnp.bfloat16)
    lowered = jnp.dot(active, w_lower, preferred_element_type=jnp.float32) + bias_rows[2].astype(
        jnp.float32
    )
    result, scaled_two, inv_two = normalize(
        normed + lowered, gain_rows[1].astype(jnp.float32), shift_rows[1].astype(jnp.float32)
    )
    states = (
        rounded,
        queries,
        keys,
        values,
        mixed,
        mixed_low,
        logsum,
        scaled_one,
        inv_one,
        normed_low,
        upward,
        active,
        scaled_two,
        inv_two,
    )
    return (result, states)


def backward_layer(grad, full, states, seq_count):
    w_attn, w_mix, w_raise, w_lower, bias_rows, bias_value, bias_raise, gain_rows, shift_rows = full
    (
        rounded,
        queries,
        keys,
        values,
        mixed,
        mixed_low,
        logsum,
        scaled_one,
        inv_one,
        normed_low,
        upward,
        active,
        scaled_two,
        inv_two,
    ) = states
    total_rows = grad.shape[0]
    row_count = total_rows // seq_count
    seq_shape = (seq_count, row_count, D)
    grad_gain_two = jnp.sum(grad * scaled_two, axis=0)
    grad_shift_two = jnp.sum(grad, axis=0)
    grad_resid = norm_back(grad, scaled_two, inv_two, gain_rows[1].astype(jnp.float32))
    grad_lowered = grad_resid.astype(jnp.bfloat16)
    grad_w_lower = jnp.einsum("tf,td->fd", active, grad_lowered, preferred_element_type=jnp.float32)
    grad_active = jnp.einsum("td,fd->tf", grad_lowered, w_lower, preferred_element_type=jnp.float32)
    unused, gelu_back = jax.vjp(exact_gelu, upward)
    grad_upward = gelu_back(grad_active)[0].astype(jnp.bfloat16)
    grad_w_raise = jnp.einsum(
        "td,tf->df", normed_low, grad_upward, preferred_element_type=jnp.float32
    )
    grad_normed = (
        jnp.einsum("tf,df->td", grad_upward, w_raise, preferred_element_type=jnp.float32)
        + grad_resid
    )
    grad_gain_one = jnp.sum(grad_normed * scaled_one, axis=0)
    grad_shift_one = jnp.sum(grad_normed, axis=0)
    grad_inner = norm_back(grad_normed, scaled_one, inv_one, gain_rows[0].astype(jnp.float32))
    grad_branch = grad_inner.astype(jnp.bfloat16)
    grad_w_mix = jnp.einsum("td,te->de", mixed_low, grad_branch, preferred_element_type=jnp.float32)
    grad_mixed = jnp.einsum(
        "te,de->td", grad_branch, w_mix, preferred_element_type=jnp.float32
    ).astype(jnp.bfloat16)
    row_delta = jnp.sum(
        (grad_mixed.astype(jnp.float32) * mixed).reshape(seq_count, row_count, HEADS, HEAD_DIM),
        axis=3,
    ).transpose(0, 2, 1)
    seq_queries = queries.reshape(seq_shape)
    seq_keys = keys.reshape(seq_shape)
    seq_values = values.reshape(seq_shape)
    seq_grad_mixed = grad_mixed.reshape(seq_shape)
    grad_queries = query_fold(seq_queries, seq_grad_mixed, logsum, row_delta, seq_keys, seq_values)
    grad_queries = merge_heads(grad_queries).astype(jnp.bfloat16)
    all_logsum, all_delta = (
        lax.all_gather(logsum, "ctx", axis=2, tiled=True),
        lax.all_gather(row_delta, "ctx", axis=2, tiled=True),
    )
    grad_keys, grad_values = key_fold(
        seq_queries, seq_grad_mixed, seq_keys, seq_values, all_logsum, all_delta
    )
    grad_keys = merge_heads(grad_keys).astype(jnp.bfloat16)
    grad_values = merge_heads(grad_values).astype(jnp.bfloat16)
    grad_project = jnp.stack([grad_queries, grad_keys, grad_values])
    grad_w_attn = jnp.einsum(
        "td,cte->dce", rounded, grad_project, preferred_element_type=jnp.float32
    )
    grad_stream = (
        jnp.einsum("cte,cde->td", grad_project, w_attn, preferred_element_type=jnp.float32)
        + grad_inner
    )
    grad_bias_rows = jnp.stack(
        [
            jnp.sum(grad_queries.astype(jnp.float32), axis=0),
            jnp.sum(grad_branch.astype(jnp.float32), axis=0),
            jnp.sum(grad_lowered.astype(jnp.float32), axis=0),
        ],
        axis=1,
    )
    grad_bias_value = jnp.sum(grad_values.astype(jnp.float32), axis=0)
    grad_bias_raise = jnp.sum(grad_upward.astype(jnp.float32), axis=0)
    local_sums = (
        grad_w_attn,
        grad_w_mix,
        grad_w_raise,
        grad_w_lower,
        grad_bias_rows,
        grad_bias_value,
        grad_bias_raise,
        jnp.stack([grad_gain_one, grad_gain_two], axis=1),
        jnp.stack([grad_shift_one, grad_shift_two], axis=1),
    )
    return (grad_stream, local_sums)


def body(inputs, w_qkv, w_out, w_up, w_down, biases, value_bias, up_bias, gains, shifts, cotangent):
    stacked = (w_qkv, w_out, w_up, w_down, biases, value_bias, up_bias, gains, shifts)
    seq_count = inputs.shape[0]
    stream = inputs.reshape(-1, D).astype(jnp.float32)
    kept_states = []
    for layer in range(LAYERS):
        shards = tuple((array[layer] for array in stacked))
        full = (
            lax.all_gather(shards[0], ("ctx", "fsdp"), axis=1, tiled=True),
            lax.all_gather(shards[1], ("ctx", "fsdp"), axis=0, tiled=True),
            lax.all_gather(shards[2], ("ctx", "fsdp"), axis=0, tiled=True),
            lax.all_gather(shards[3], ("ctx", "fsdp"), axis=0, tiled=True),
            lax.all_gather(shards[4], ("ctx", "fsdp"), axis=1, tiled=True),
            lax.all_gather(shards[5], ("ctx", "fsdp"), axis=0, tiled=True),
            lax.all_gather(shards[6], ("ctx", "fsdp"), axis=0, tiled=True),
            lax.all_gather(shards[7], ("ctx", "fsdp"), axis=1, tiled=True),
            lax.all_gather(shards[8], ("ctx", "fsdp"), axis=1, tiled=True),
        )
        stream, states = forward_layer(stream, full, seq_count)
        kept_states.append(states)
    output = stream.astype(jnp.bfloat16).reshape(inputs.shape)
    grad = cotangent.reshape(-1, D).astype(jnp.float32)
    layer_grads = [None] * LAYERS
    for layer in reversed(range(LAYERS)):
        shards = tuple((array[layer] for array in stacked))
        full = (
            lax.all_gather(shards[0], ("ctx", "fsdp"), axis=1, tiled=True),
            lax.all_gather(shards[1], ("ctx", "fsdp"), axis=0, tiled=True),
            lax.all_gather(shards[2], ("ctx", "fsdp"), axis=0, tiled=True),
            lax.all_gather(shards[3], ("ctx", "fsdp"), axis=0, tiled=True),
            lax.all_gather(shards[4], ("ctx", "fsdp"), axis=1, tiled=True),
            lax.all_gather(shards[5], ("ctx", "fsdp"), axis=0, tiled=True),
            lax.all_gather(shards[6], ("ctx", "fsdp"), axis=0, tiled=True),
            lax.all_gather(shards[7], ("ctx", "fsdp"), axis=1, tiled=True),
            lax.all_gather(shards[8], ("ctx", "fsdp"), axis=1, tiled=True),
        )
        grad, local_sums = backward_layer(grad, full, kept_states[layer], seq_count)
        partial_sums = (
            lax.psum_scatter(local_sums[0], "ctx", scatter_dimension=0, tiled=True),
            lax.psum_scatter(local_sums[1], "ctx", scatter_dimension=0, tiled=True),
            lax.psum_scatter(local_sums[2], "ctx", scatter_dimension=0, tiled=True),
            lax.psum_scatter(local_sums[3], "ctx", scatter_dimension=0, tiled=True),
            lax.psum_scatter(local_sums[4], "ctx", scatter_dimension=0, tiled=True),
            lax.psum_scatter(local_sums[5], "ctx", scatter_dimension=0, tiled=True),
            lax.psum_scatter(local_sums[6], "ctx", scatter_dimension=0, tiled=True),
            lax.psum_scatter(local_sums[7], "ctx", scatter_dimension=0, tiled=True),
            lax.psum_scatter(local_sums[8], "ctx", scatter_dimension=0, tiled=True),
        )
        reduced = (
            lax.psum_scatter(
                partial_sums[0].astype(jnp.bfloat16), "fsdp", scatter_dimension=0, tiled=True
            ).astype(jnp.float32),
            lax.psum_scatter(
                partial_sums[1].astype(jnp.bfloat16), "fsdp", scatter_dimension=0, tiled=True
            ).astype(jnp.float32),
            lax.psum_scatter(
                partial_sums[2].astype(jnp.bfloat16), "fsdp", scatter_dimension=0, tiled=True
            ).astype(jnp.float32),
            lax.psum_scatter(
                partial_sums[3].astype(jnp.bfloat16), "fsdp", scatter_dimension=0, tiled=True
            ).astype(jnp.float32),
            lax.psum_scatter(
                partial_sums[4].astype(jnp.bfloat16), "fsdp", scatter_dimension=0, tiled=True
            ).astype(jnp.float32),
            lax.psum_scatter(
                partial_sums[5].astype(jnp.bfloat16), "fsdp", scatter_dimension=0, tiled=True
            ).astype(jnp.float32),
            lax.psum_scatter(
                partial_sums[6].astype(jnp.bfloat16), "fsdp", scatter_dimension=0, tiled=True
            ).astype(jnp.float32),
            lax.psum_scatter(
                partial_sums[7].astype(jnp.bfloat16), "fsdp", scatter_dimension=0, tiled=True
            ).astype(jnp.float32),
            lax.psum_scatter(
                partial_sums[8].astype(jnp.bfloat16), "fsdp", scatter_dimension=0, tiled=True
            ).astype(jnp.float32),
        )
        layer_grads[layer] = (
            reduced[0].transpose(1, 0, 2),
            reduced[1],
            reduced[2],
            reduced[3],
            reduced[4].T,
            reduced[5],
            reduced[6],
            reduced[7].T,
            reduced[8].T,
        )
    grad_inputs = grad.astype(jnp.bfloat16).reshape(inputs.shape)
    return (
        output,
        grad_inputs,
        jnp.stack([member[0] for member in layer_grads]),
        jnp.stack([member[1] for member in layer_grads]),
        jnp.stack([member[2] for member in layer_grads]),
        jnp.stack([member[3] for member in layer_grads]),
        jnp.stack([member[4] for member in layer_grads]),
        jnp.stack([member[5] for member in layer_grads]),
        jnp.stack([member[6] for member in layer_grads]),
        jnp.stack([member[7] for member in layer_grads]),
        jnp.stack([member[8] for member in layer_grads]),
    )


def solution(mesh):
    return jax.shard_map(
        body,
        mesh=mesh,
        in_specs=(
            P("fsdp", "ctx", None),
            P(None, None, ("ctx", "fsdp"), None),
            P(None, ("ctx", "fsdp"), None),
            P(None, ("ctx", "fsdp"), None),
            P(None, ("ctx", "fsdp"), None),
            P(None, None, ("ctx", "fsdp")),
            P(None, ("ctx", "fsdp")),
            P(None, ("ctx", "fsdp")),
            P(None, None, ("ctx", "fsdp")),
            P(None, None, ("ctx", "fsdp")),
            P("fsdp", "ctx", None),
        ),
        out_specs=(
            P("fsdp", "ctx", None),
            P("fsdp", "ctx", None),
            P(None, None, ("ctx", "fsdp"), None),
            P(None, ("ctx", "fsdp"), None),
            P(None, ("ctx", "fsdp"), None),
            P(None, ("ctx", "fsdp"), None),
            P(None, None, ("ctx", "fsdp")),
            P(None, ("ctx", "fsdp")),
            P(None, ("ctx", "fsdp")),
            P(None, None, ("ctx", "fsdp")),
            P(None, None, ("ctx", "fsdp")),
        ),
        check_vma=False,
    )
```

profile of v0, /device:TPU:1, one launch (start us, length us, event | category | flops | bytes accessed | tf_op | source)
XLA Modules:
  0.0 2537.6 jit_solution(10314052117168391485)
XLA Ops:
  11.3 41.8 %all-reduce.21 = (bf16[3072]{0:T(1024)(128)(2,1)}, bf16[3072]{0:T(1024)(128)(2,1)S(1)}, bf16[768]{0:T(1024)(128)(2,1)S(1)}, bf16[768]{0:T(1024)(128)(2,1)}) all-reduce(bf16[3072]{0:T(1024)(128)(2,1)S(1)} %dynamic-update-slice.3, bf16[3072]{0:T(1024)(128)(2,1)S(1)} %dynamic-update-slice.1, ...), channel_id=18, replica_groups=mesh['ctx'=8,'fsdp'=4] {'ctx','fsdp'}, use_global_device_ids=true, to_apply=%add.3 | all-reduce | flops 7680 | bytes 30720
  53.1 21.2 all-gather.51.cloned.1.call-done
  83.9 41.2 %all-gather.1 = bf16[1,3,768]{1,0,2:T(2,128)(2,1)S(1)} all-gather(bf16[1,3,24]{1,0,2:T(2,128)(2,1)S(1)} %copy.416), channel_id=3, replica_groups=mesh['ctx'=8,'fsdp'=4] {'ctx','fsdp'}, dimensions={2}, use_global_device_ids=true | all-gather | bytes 4752 | tf_op jit(solution)/shard_map/all_gather | solution.py:341
  125.1 7.8 fusion.168
  134.2 38.7 %all-gather.5 = bf16[1,2,768]{1,0,2:T(2,128)(2,1)S(1)} all-gather(bf16[1,2,24]{1,0,2:T(2,128)(2,1)S(1)} %copy.418), channel_id=7, replica_groups=mesh['ctx'=8,'fsdp'=4] {'ctx','fsdp'}, dimensions={2}, use_global_device_ids=true | all-gather | bytes 3168 | tf_op jit(solution)/shard_map/all_gather | solution.py:345
  173.0 39.4 %all-gather.4 = bf16[1,2,768]{1,0,2:T(2,128)(2,1)S(1)} all-gather(bf16[1,2,24]{1,0,2:T(2,128)(2,1)S(1)} %copy.417), channel_id=6, replica_groups=mesh['ctx'=8,'fsdp'=4] {'ctx','fsdp'}, dimensions={2}, use_global_device_ids=true | all-gather | bytes 3168 | tf_op jit(solution)/shard_map/all_gather | solution.py:344
  236.4 54.0 %all-gather.55.cloned.1.call-done = bf16[1,768,3072]{2,1,0:T(8,128)(2,1)} async-done(((bf16[1,24,3072]{2,1,0:T(8,128)(2,1)}), bf16[1,768,3072]{2,1,0:T(8,128)(2,1)}) %all-gather.55.cloned.1.call-update) | async-done | bytes 4718608 | tf_op jit(solution)/shard_map/all_gather | solution.py:339
  290.4 8.3 multiply_convert_fusion.5
  298.8 57.4 %all-gather.57.cloned.1.call-done = bf16[1,3072,768]{2,1,0:T(8,128)(2,1)} async-done(((bf16[1,96,768]{2,1,0:T(8,128)(2,1)}), bf16[1,3072,768]{2,1,0:T(8,128)(2,1)}) %all-gather.57.cloned.1.call-update) | async-done | bytes 4718608 | tf_op jit(solution)/shard_map/all_gather | solution.py:340
  359.6 59.0 %all-gather.59.cloned.1.call-done = bf16[1,3,768,768]{3,2,1,0:T(8,128)(2,1)} async-done(((bf16[1,3,24,768]{3,2,1,0:T(8,128)(2,1)}), bf16[1,3,768,768]{3,2,1,0:T(8,128)(2,1)}) %all-gather.59.cloned.1.call-update) | async-done | bytes 3538960 | tf_op jit(solution)/shard_map/all_gather | solution.py:337
  426.4 41.7 %all-gather.10 = bf16[1,3,768]{1,0,2:T(2,128)(2,1)S(1)} all-gather(bf16[1,3,24]{1,0,2:T(2,128)(2,1)S(1)} %copy.419), channel_id=12, replica_groups=mesh['ctx'=8,'fsdp'=4] {'ctx','fsdp'}, dimensions={2}, use_global_device_ids=true | all-gather | bytes 4752 | tf_op jit(solution)/shard_map/all_gather | solution.py:341
  468.1 7.8 fusion.161
  476.2 38.5 %all-gather.13 = bf16[1,2,768]{1,0,2:T(2,128)(2,1)S(1)} all-gather(bf16[1,2,24]{1,0,2:T(2,128)(2,1)S(1)} %copy.420), channel_id=15, replica_groups=mesh['ctx'=8,'fsdp'=4] {'ctx','fsdp'}, dimensions={2}, use_global_device_ids=true | all-gather | bytes 3168 | tf_op jit(solution)/shard_map/all_gather | solution.py:344
  520.6 39.6 %all-gather.14 = bf16[1,2,768]{1,0,2:T(2,128)(2,1)S(1)} all-gather(bf16[1,2,24]{1,0,2:T(2,128)(2,1)S(1)} %copy.421), channel_id=16, replica_groups=mesh['ctx'=8,'fsdp'=4] {'ctx','fsdp'}, dimensions={2}, use_global_device_ids=true | all-gather | bytes 3168 | tf_op jit(solution)/shard_map/all_gather | solution.py:345
  586.2 48.3 %all-gather.63.cloned.1.call-done = bf16[1,768,3072]{2,1,0:T(8,128)(2,1)} async-done(((bf16[1,24,3072]{2,1,0:T(8,128)(2,1)}), bf16[1,768,3072]{2,1,0:T(8,128)(2,1)}) %all-gather.63.cloned.1.call-update) | async-done | bytes 4718608 | tf_op jit(solution)/shard_map/all_gather | solution.py:339
  634.6 8.4 multiply_convert_fusion.4
  643.0 56.8 %all-gather.65.cloned.1.call-done = bf16[1,3072,768]{2,1,0:T(8,128)(2,1)} async-done(((bf16[1,96,768]{2,1,0:T(8,128)(2,1)}), bf16[1,3072,768]{2,1,0:T(8,128)(2,1)}) %all-gather.65.cloned.1.call-update) | async-done | bytes 4718608 | tf_op jit(solution)/shard_map/all_gather | solution.py:340
  705.7 5.5 convert_reduce_fusion
  741.9 26.4 %all_gather.129 = f32[2,12,512]{1,0,2:T(2,128)S(1)} all-gather(f32[2,12,64]{1,0,2:T(2,128)S(1)} %copy-done.52), channel_id=1, replica_groups=mesh['ctx'=8,'fsdp'=4] {'ctx'}, dimensions={2}, use_global_device_ids=true | all-gather | bytes 55296 | tf_op jit(solution)/shard_map/all_gather | solution.py:290
  769.1 26.9 %all_gather.127 = f32[2,12,512]{1,0,2:T(2,128)S(1)} all-gather(f32[2,12,64]{1,0,2:T(2,128)S(1)} %copy-done.51), channel_id=1, replica_groups=mesh['ctx'=8,'fsdp'=4] {'ctx'}, dimensions={2}, use_global_device_ids=true | all-gather | bytes 55296 | tf_op jit(solution)/shard_map/all_gather | solution.py:289
  819.0 5.3 convert_reduce_fusion.1
  838.9 8.0 copy.414
  851.4 26.6 %all_gather.131 = f32[2,12,512]{1,0,2:T(2,128)S(1)} all-gather(f32[2,12,64]{1,0,2:T(2,128)S(1)} %copy.338), channel_id=1, replica_groups=mesh['ctx'=8,'fsdp'=4] {'ctx'}, dimensions={2}, use_global_device_ids=true | all-gather | bytes 55296 | tf_op jit(solution)/shard_map/all_gather | solution.py:289
  894.7 5.8 convert_reduce_fusion.5
  904.5 27.7 %all_gather.133 = f32[2,12,512]{1,0,2:T(2,128)} all-gather(f32[2,12,64]{1,0,2:T(2,128)} %copy.343), channel_id=1, replica_groups=mesh['ctx'=8,'fsdp'=4] {'ctx'}, dimensions={2}, use_global_device_ids=true | all-gather | bytes 55296 | tf_op jit(solution)/shard_map/all_gather | solution.py:290
  954.4 8.1 copy.412
  995.9 39.1 %reduce-scatter.43.cloned.1.call-done = f32[96,768]{1,0:T(8,128)} async-done(((f32[768,768]{1,0:T(8,128)}), f32[96,768]{1,0:T(8,128)}) %reduce-scatter.43.cloned.1.call-update) | async-done | bytes 294928 | tf_op jit(solution)/shard_map/reduce_scatter | solution.py:368
  1036.7 130.1 %reduce-scatter.69.cloned.1.call-done = f32[96,2304]{1,0:T(8,128)} async-done(((f32[768,2304]{1,0:T(8,128)}), f32[96,2304]{1,0:T(8,128)}) %reduce-scatter.69.cloned.1.call-update) | async-done | bytes 884752
  1169.7 129.2 %reduce-scatter.67.cloned.1.call-done = f32[96,2304]{1,0:T(8,128)} async-done(((f32[768,2304]{1,0:T(8,128)}), f32[96,2304]{1,0:T(8,128)}) %reduce-scatter.67.cloned.1.call-update) | async-done | bytes 884752
  1301.9 164.1 %reduce-scatter.55.cloned.1.call-done = f32[96,3072]{1,0:T(8,128)} async-done(((f32[768,3072]{1,0:T(8,128)}), f32[96,3072]{1,0:T(8,128)}) %reduce-scatter.55.cloned.1.call-update) | async-done | bytes 1179664 | tf_op jit(solution)/shard_map/reduce_scatter | solution.py:369
  1468.3 163.9 %reduce-scatter.51.cloned.1.call-done = f32[96,3072]{1,0:T(8,128)} async-done(((f32[768,3072]{1,0:T(8,128)}), f32[96,3072]{1,0:T(8,128)}) %reduce-scatter.51.cloned.1.call-update) | async-done | bytes 1179664 | tf_op jit(solution)/shard_map/reduce_scatter | solution.py:369
  1638.2 55.8 %reduce-scatter.77.cloned.1.call-done = f32[96,2]{1,0:T(8,128)} async-done(((f32[768,2]{1,0:T(8,128)}), f32[96,2]{1,0:T(8,128)}) %reduce-scatter.77.cloned.1.call-update) | async-done | bytes 784
  1694.9 62.7 %reduce-scatter.81.cloned.1.call-done = f32[96,2]{1,0:T(8,128)} async-done(((f32[768,2]{1,0:T(8,128)}), f32[96,2]{1,0:T(8,128)}) %reduce-scatter.81.cloned.1.call-update) | async-done | bytes 784
  1758.5 62.8 %reduce-scatter.73.cloned.1.call-done = f32[96,3]{1,0:T(8,128)} async-done(((f32[768,3]{1,0:T(8,128)}), f32[96,3]{1,0:T(8,128)}) %reduce-scatter.73.cloned.1.call-update) | async-done | bytes 1168
  1822.3 62.6 %reduce-scatter.75.cloned.1.call-done = f32[96,2]{1,0:T(8,128)} async-done(((f32[768,2]{1,0:T(8,128)}), f32[96,2]{1,0:T(8,128)}) %reduce-scatter.75.cloned.1.call-update) | async-done | bytes 784
  1885.7 62.7 %reduce-scatter.79.cloned.1.call-done = f32[96,2]{1,0:T(8,128)} async-done(((f32[768,2]{1,0:T(8,128)}), f32[96,2]{1,0:T(8,128)}) %reduce-scatter.79.cloned.1.call-update) | async-done | bytes 784
  1949.3 62.8 %reduce-scatter.71.cloned.1.call-done = f32[96,3]{1,0:T(8,128)} async-done(((f32[768,3]{1,0:T(8,128)}), f32[96,3]{1,0:T(8,128)}) %reduce-scatter.71.cloned.1.call-update) | async-done | bytes 1168
  2013.1 29.5 %all-reduce.20 = (bf16[768]{0:T(1024)(128)(2,1)S(1)}, bf16[768]{0:T(1024)(128)(2,1)S(1)}, bf16[3072]{0:T(1024)(128)(2,1)S(1)}, bf16[3072]{0:T(1024)(128)(2,1)S(1)}) all-reduce(f32[768]{0:T(1024)S(1)} %reduce_sum.383, f32[768]{0:T(1024)S(1)} %reduce_sum.381, ...), channel_id=42, replica_groups=mesh['ctx'=8,'fsdp'=4] {'ctx'}, use_global_device_ids=true, to_apply=%region_52.53.clone | all-reduce | flops 7680 | bytes 46080
  2042.9 15.5 all-reduce.22
  2059.7 120.7 %reduce-scatter.63.cloned.1.call-done = f32[384,768]{1,0:T(8,128)} async-done(((f32[3072,768]{1,0:T(8,128)}), f32[384,768]{1,0:T(8,128)}) %reduce-scatter.63.cloned.1.call-update) | async-done | bytes 1179664 | tf_op jit(solution)/shard_map/reduce_scatter | solution.py:370
  2189.0 157.4 %reduce-scatter.59.cloned.1.call-done = f32[384,768]{1,0:T(8,128)} async-done(((f32[3072,768]{1,0:T(8,128)}), f32[384,768]{1,0:T(8,128)}) %reduce-scatter.59.cloned.1.call-update) | async-done | bytes 1179664 | tf_op jit(solution)/shard_map/reduce_scatter | solution.py:370
  2352.9 14.7 reduce-scatter.49.cloned.1.call-done
  2367.7 22.1 reduce-scatter.45.cloned.1.call-done
  2391.2 39.3 %all-reduce.26.cloned.1.call-done = (bf16[96,3,768]{2,1,0:T(4,128)(2,1)}, bf16[96,3,768]{2,1,0:T(4,128)(2,1)}) async-done(((bf16[96,3,768]{2,1,0:T(4,128)(2,1)}, bf16[96,3,768]{2,1,0:T(4,128)(2,1)}), (bf16[96,3,768]{2,1,0:T(4,128)(2,1)}, bf16[96,3,768]{2,1,0:T(4,128)(2,1)})) %all-reduce.26.cloned.1.call-update) | async-done | bytes 884752
  2433.3 22.0 reduce-scatter.57.cloned.1.call-done
  2455.3 24.6 reduce-scatter.53.cloned.1.call-done
  2481.7 22.6 reduce-scatter.65.cloned.1.call-done
  2504.3 24.4 reduce-scatter.61.cloned.1.call-done
  (587 shorter events, 279.5 us)
Async XLA Ops:
  7.2 67.1 %all-gather.51.cloned.1.call-start = ((), (), s32[]{:S(2)}) async-start(), calls=%async_computation.40 | async-start | bytes 3649536 | tf_op jit(solution)/shard_map/all_gather | solution.py:337
  8.9 214.6 %all-gather.37.cloned.1.call-start = ((), (), s32[]{:S(2)}) async-start(), calls=%async_computation.21 | async-start | bytes 1769472 | tf_op jit(solution)/shard_map/all_gather | solution.py:62
  77.1 144.5 %copy-start.28 = (f32[1,128,768]{2,1,0:T(8,128)}, f32[1,128,768]{2,1,0:T(8,128)S(1)}, u32[]{:S(2)}) copy-start(f32[1,128,768]{2,1,0:T(8,128)S(1)} %get-tuple-element.285) | copy-start | bytes 1179652
  78.6 146.7 %all-gather.35.cloned.1.call-start = ((), (), s32[]{:S(2)}) async-start(), calls=%async_computation.20 | async-start | bytes 1769472 | tf_op jit(solution)/shard_map/all_gather | solution.py:61
  79.4 154.9 %all-gather.53.cloned.1.call-start = ((), (), s32[]{:S(2)}) async-start(), calls=%async_computation.41 | async-start | bytes 1216512 | tf_op jit(solution)/shard_map/all_gather | solution.py:338
  80.1 210.3 %all-gather.55.cloned.1.call-start = ((), (), s32[]{:S(2)}) async-start(), calls=%async_computation.42 | async-start | bytes 4866048 | tf_op jit(solution)/shard_map/all_gather | solution.py:339
  81.0 275.2 %all-gather.57.cloned.1.call-start = ((), (), s32[]{:S(2)}) async-start(), calls=%async_computation.43 | async-start | bytes 4866048 | tf_op jit(solution)/shard_map/all_gather | solution.py:340
  81.8 336.9 %all-gather.59.cloned.1.call-start = ((), (), s32[]{:S(2)}) async-start(), calls=%async_computation.44 | async-start | bytes 3649536 | tf_op jit(solution)/shard_map/all_gather | solution.py:337
  82.5 486.4 %all-gather.39.cloned.1.call-start = ((), (), s32[]{:S(2)}) async-start(), calls=%async_computation.22 | async-start | bytes 1769472 | tf_op jit(solution)/shard_map/all_gather | solution.py:61
  217.0 201.7 %copy-start.56 = (f32[768]{0:T(1024)}, f32[768]{0:T(1024)S(1)}, u32[]{:S(2)}) copy-start(f32[768]{0:T(1024)S(1)} %get-tuple-element.244) | copy-start | bytes 9220
  422.2 154.1 %all-gather.41.cloned.1.call-start = ((), (), s32[]{:S(2)}) async-start(), calls=%async_computation.23 | async-start | bytes 1769472 | tf_op jit(solution)/shard_map/all_gather | solution.py:62
  423.8 160.3 %all-gather.61.cloned.1.call-start = ((), (), s32[]{:S(2)}) async-start(), calls=%async_computation.45 | async-start | bytes 1216512 | tf_op jit(solution)/shard_map/all_gather | solution.py:338
  424.4 210.2 %all-gather.63.cloned.1.call-start = ((), (), s32[]{:S(2)}) async-start(), calls=%async_computation.46 | async-start | bytes 4866048 | tf_op jit(solution)/shard_map/all_gather | solution.py:339
  425.1 274.7 %all-gather.65.cloned.1.call-start = ((), (), s32[]{:S(2)}) async-start(), calls=%async_computation.47 | async-start | bytes 4866048 | tf_op jit(solution)/shard_map/all_gather | solution.py:340
  425.7 371.1 %all-gather.43.cloned.1.call-start = ((), (), s32[]{:S(2)}) async-start(), calls=%async_computation.24 | async-start | bytes 1769472 | tf_op jit(solution)/shard_map/all_gather | solution.py:141
  568.4 233.1 %all-gather.45.cloned.1.call-start = ((), (), s32[]{:S(2)}) async-start(), calls=%async_computation.25 | async-start | bytes 1769472 | tf_op jit(solution)/shard_map/all_gather | solution.py:142
  586.0 127.6 %copy-start.3 = (f32[128,768]{1,0:T(8,128)}, f32[128,768]{1,0:T(8,128)S(1)}, u32[]{:S(2)}) copy-start(f32[128,768]{1,0:T(8,128)S(1)} %get-tuple-element.320) | copy-start | bytes 1179652
  586.0 127.6 %copy-start.73 = (f32[128]{0:T(128)}, f32[128]{0:T(128)S(1)}, u32[]{:S(2)}) copy-start(f32[128]{0:T(128)S(1)} %broadcast_multiply_fusion.9) | copy-start | bytes 1540
  716.5 162.3 %all-gather.47.cloned.1.call-start = ((), (), s32[]{:S(2)}) async-start(), calls=%async_computation.26 | async-start | bytes 1769472 | tf_op jit(solution)/shard_map/all_gather | solution.py:141
  717.4 218.3 %all-gather.49.cloned.1.call-start = ((), (), s32[]{:S(2)}) async-start(), calls=%async_computation.27 | async-start | bytes 1769472 | tf_op jit(solution)/shard_map/all_gather | solution.py:142
  829.4 164.8 %reduce-scatter.47.cloned.1.call-start = ((), (), s32[]{:S(2)}) async-start(), calls=%async_computation.30 | async-start | bytes 2654208 | tf_op jit(solution)/shard_map/reduce_scatter | solution.py:368
  831.3 203.7 %reduce-scatter.43.cloned.1.call-start = ((), (), s32[]{:S(2)}) async-start(), calls=%async_computation.28 | async-start | bytes 2654208 | tf_op jit(solution)/shard_map/reduce_scatter | solution.py:368
  834.2 332.6 %reduce-scatter.69.cloned.1.call-start = ((), (), s32[]{:S(2)}) async-start(), calls=%async_computation.49 | async-start | bytes 7962624
  846.9 452.0 %reduce-scatter.67.cloned.1.call-start = ((), (), s32[]{:S(2)}) async-start(), calls=%async_computation.48 | async-start | bytes 7962624
  962.5 503.5 %reduce-scatter.55.cloned.1.call-start = ((), (), s32[]{:S(2)}) async-start(), calls=%async_computation.34 | async-start | bytes 10616832 | tf_op jit(solution)/shard_map/reduce_scatter | solution.py:369
  968.9 663.3 %reduce-scatter.51.cloned.1.call-start = ((), (), s32[]{:S(2)}) async-start(), calls=%async_computation.32 | async-start | bytes 10616832 | tf_op jit(solution)/shard_map/reduce_scatter | solution.py:369
  975.4 718.6 %reduce-scatter.77.cloned.1.call-start = ((), (), s32[]{:S(2)}) async-start(), calls=%async_computation.53 | async-start | bytes 442368
  977.0 780.6 %reduce-scatter.81.cloned.1.call-start = ((), (), s32[]{:S(2)}) async-start(), calls=%async_computation.55 | async-start | bytes 442368
  978.2 843.1 %reduce-scatter.73.cloned.1.call-start = ((), (), s32[]{:S(2)}) async-start(), calls=%async_computation.51 | async-start | bytes 442368
  979.3 905.6 %reduce-scatter.75.cloned.1.call-start = ((), (), s32[]{:S(2)}) async-start(), calls=%async_computation.52 | async-start | bytes 442368
  980.4 968.0 %reduce-scatter.79.cloned.1.call-start = ((), (), s32[]{:S(2)}) async-start(), calls=%async_computation.54 | async-start | bytes 442368
  981.6 1030.5 %reduce-scatter.71.cloned.1.call-start = ((), (), s32[]{:S(2)}) async-start(), calls=%async_computation.50 | async-start | bytes 442368
  982.6 1197.8 %reduce-scatter.63.cloned.1.call-start = ((), (), s32[]{:S(2)}) async-start(), calls=%async_computation.38 | async-start | bytes 10616832 | tf_op jit(solution)/shard_map/reduce_scatter | solution.py:370
  987.8 1358.6 %reduce-scatter.59.cloned.1.call-start = ((), (), s32[]{:S(2)}) async-start(), calls=%async_computation.36 | async-start | bytes 10616832 | tf_op jit(solution)/shard_map/reduce_scatter | solution.py:370
  994.1 1373.6 %reduce-scatter.49.cloned.1.call-start = ((), (), s32[]{:S(2)}) async-start(), calls=%async_computation.31 | async-start | bytes 184320 | tf_op jit(solution)/shard_map/reduce_scatter | solution.py:381
  995.8 1394.0 %reduce-scatter.45.cloned.1.call-start = ((), (), s32[]{:S(2)}) async-start(), calls=%async_computation.29 | async-start | bytes 184320 | tf_op jit(solution)/shard_map/reduce_scatter | solution.py:381
  1036.6 1393.9 %all-reduce.26.cloned.1.call-start = ((), (), s32[]{:S(2)}) async-start(), calls=%async_computation.56 | async-start | bytes 2359296
  1301.8 1153.4 %reduce-scatter.57.cloned.1.call-start = ((), (), s32[]{:S(2)}) async-start(), calls=%async_computation.35 | async-start | bytes 737280 | tf_op jit(solution)/shard_map/reduce_scatter | solution.py:384
  1468.2 166.3 %copy-start.119 = (u32[32]{0:T(128)S(1)}, u32[32]{0:T(128)}, u32[]{:S(2)}) copy-start(u32[32]{0:T(128)} %constant.183) | copy-start | bytes 388
  1468.2 166.9 %copy-start.118 = (u32[32]{0:T(128)S(1)}, u32[32]{0:T(128)}, u32[]{:S(2)}) copy-start(u32[32]{0:T(128)} %constant.199) | copy-start | bytes 388
  1468.2 354.0 %copy-start.65 = (f32[12,64]{1,0:T(8,128)S(1)}, f32[12,64]{1,0:T(8,128)}, u32[]{:S(2)}) copy-start(f32[12,64]{1,0:T(8,128)} %get-tuple-element.335) | copy-start | bytes 9220
  1468.2 544.8 %copy-start.66 = (f32[12,64]{1,0:T(8,128)S(1)}, f32[12,64]{1,0:T(8,128)}, u32[]{:S(2)}) copy-start(f32[12,64]{1,0:T(8,128)} %get-tuple-element.337) | copy-start | bytes 9220
  1468.2 544.8 %copy-start.102 = (f32[3072]{0:T(1024)S(1)}, f32[3072]{0:T(1024)}, u32[]{:S(2)}) copy-start(f32[3072]{0:T(1024)} %get-tuple-element.339) | copy-start | bytes 36868
  1468.2 544.8 %copy-start.103 = (f32[3072]{0:T(1024)S(1)}, f32[3072]{0:T(1024)}, u32[]{:S(2)}) copy-start(f32[3072]{0:T(1024)} %get-tuple-element.341) | copy-start | bytes 36868
  1468.3 1011.6 %reduce-scatter.53.cloned.1.call-start = ((), (), s32[]{:S(2)}) async-start(), calls=%async_computation.33 | async-start | bytes 737280 | tf_op jit(solution)/shard_map/reduce_scatter | solution.py:384
  1634.4 869.9 %reduce-scatter.65.cloned.1.call-start = ((), (), s32[]{:S(2)}) async-start(), calls=%async_computation.39 | async-start | bytes 737280 | tf_op jit(solution)/shard_map/reduce_scatter | solution.py:387
  2180.4 169.4 %copy-start.5 = (bf16[1,3,768,768]{3,2,1,0:T(8,128)(2,1)S(1)}, bf16[1,3,768,768]{3,2,1,0:T(8,128)(2,1)}, u32[]{:S(2)}) copy-start(bf16[1,3,768,768]{3,2,1,0:T(8,128)(2,1)} %all-gather.51.cloned.1.call-done) | copy-start | bytes 10616836
  2182.7 346.0 %reduce-scatter.61.cloned.1.call-start = ((), (), s32[]{:S(2)}) async-start(), calls=%async_computation.37 | async-start | bytes 737280 | tf_op jit(solution)/shard_map/reduce_scatter | solution.py:387
  (115 other events, 1860.5 us)
Sparse Core Ops, SparseCore 0:
  11.4 62.7 all-gather.50
  78.7 42.1 all-gather.36
  123.1 43.8 all-gather.34
  169.8 54.7 all-gather.52
  227.9 62.4 all-gather.54
  293.7 62.3 all-gather.56
  359.6 59.0 all-gather.58
  422.3 41.7 all-gather.38
  466.9 43.8 all-gather.40
  513.6 54.9 all-gather.60
  572.0 62.5 all-gather.62
  637.3 62.3 all-gather.64
  701.9 41.9 all-gather.42
  746.5 48.7 all-gather.44
  797.4 43.8 all-gather.46
  843.9 46.3 all-gather.48
  893.6 69.9 reduce-scatter.46
  967.0 67.9 reduce-scatter.42
  1038.7 128.1 reduce-scatter.68
  1170.8 128.0 reduce-scatter.66
  1302.5 163.4 reduce-scatter.54
  1469.6 162.5 reduce-scatter.50
  1635.5 58.4 reduce-scatter.76
  1697.1 60.4 reduce-scatter.80
  1760.9 60.3 reduce-scatter.72
  1824.4 60.3 reduce-scatter.74
  1888.0 60.4 reduce-scatter.78
  1951.7 60.3 reduce-scatter.70
  2015.7 164.6 reduce-scatter.62
  2183.8 162.5 reduce-scatter.58
  2349.5 18.1 reduce-scatter.48
  2370.1 19.6 reduce-scatter.44
  2392.6 37.8 all-reduce.25
  2433.0 22.1 reduce-scatter.56
  2457.8 22.0 reduce-scatter.52
  2482.2 22.0 reduce-scatter.64
  2506.6 22.0 reduce-scatter.60
where the time goes:
time: 2550 us; the launch traced here: 2540 us
  waiting for transfers between devices  1740 us (68%)
  blocking collectives  434 us (17%)
  local copies, waits for them, and re-layouts  132 us (5%)
  matrix products  127 us (5%)
  other arithmetic  79.7 us (3%)
    unnamed x46, waiting for transfers between devices  671 us
    reduce_scatter x2, waiting for transfers between devices, body(): lax.psum_scatter(local_sums[2], 'ctx', scatter_dimension=0, tiled=True)  328 us
    reduce_scatter x2, waiting for transfers between devices, body(): lax.psum_scatter(local_sums[3], 'ctx', scatter_dimension=0, tiled=True)  278 us
    all_gather x2, waiting for transfers between devices, body(): lax.all_gather(shards[3], ('ctx', 'fsdp'), axis=0, tiled=True)  114 us
    all_gather x2, waiting for transfers between devices, body(): lax.all_gather(shards[2], ('ctx', 'fsdp'), axis=0, tiled=True)  102 us
    unnamed x3, blocking collectives  86.8 us
    all_gather x2, blocking collectives, body(): lax.all_gather(shards[4], ('ctx', 'fsdp'), axis=1, tiled=True)  82.9 us
    all_gather x2, waiting for transfers between devices, body(): lax.all_gather(shards[0], ('ctx', 'fsdp'), axis=1, tiled=True)  80.2 us
  transfers between devices with their start and end apart: 37, of which 26 were waited for; matrix products, arithmetic and copies ran while one was open for 13% of the time, Pallas kernels for 0%

commit v1 on v0

--- a/solution.py
+++ b/solution.py
@@ -1,12 +1,1262 @@
+import functools
+import types
+
 import jax
 import jax.numpy as jnp
 from jax import lax
+from jax.experimental import pallas as pl
+from jax.experimental.pallas import tpu as pltpu
 from jax.sharding import PartitionSpec as P
 
 D = 768
 HEADS = 12
 HEAD_DIM = 64
 LAYERS = 2
+KERNEL_VMEM = 63 * 2**20
+
+
+BF = jnp.bfloat16
+F32 = jnp.float32
+MESH = pl.DeviceIdType.MESH
+MEMBERS = 4
+LOCAL_HEADS = HEADS // MEMBERS
+PACK = 640
+SLOT = 64
+PIECE = 64
+
+
+def dot_nn(left, right):
+    return lax.dot_general(left, right, (((1,), (0,)), ((), ())), preferred_element_type=F32)
+
+
+def dot_nt(left, right):
+    return lax.dot_general(left, right, (((1,), (1,)), ((), ())), preferred_element_type=F32)
+
+
+def dot_tn(left, right):
+    return lax.dot_general(left, right, (((0,), (0,)), ((), ())), preferred_element_type=F32)
+
+
+def dot_exact(left, right):
+    return lax.dot_general(
+        left,
+        right,
+        (((1,), (0,)), ((), ())),
+        precision=lax.Precision.HIGHEST,
+        preferred_element_type=F32,
+    )
+
+
+def packed_lanes(shape, axis):
+    lane = lax.broadcasted_iota(jnp.int32, shape, axis)
+    slot = lane >> 6
+    head = jnp.where(slot >= 6, 2, slot & 1)
+    is_query = (slot < 2) | (slot == 6)
+    is_value = (slot == 4) | (slot == 5) | (slot == 8)
+    return (head * HEAD_DIM + (lane & 63), is_query, is_value)
+
+
+def scratch_layout(nz, ny, rows, half, d_rows, f_rows):
+    dma = pltpu.SemaphoreType.DMA
+    two = 2 * d_rows
+    ff = nz * ny * f_rows
+    vm = pltpu.VMEM
+    return dict(
+        wq=vm((LAYERS, nz, 2, ny, two, PACK), BF),
+        wu=vm((LAYERS, nz, 2, ny, two, ff), BF),
+        wd=vm((LAYERS, nz, ny, f_rows, D), BF),
+        wog=vm((nz, ny, two, D), BF),
+        wo=vm((LAYERS, 256, D), BF),
+        smg=vm((nz, ny, MEMBERS, 32, 128), BF),
+        qs=vm((MEMBERS, two, PACK), BF),
+        us=vm((MEMBERS, two, ff), BF),
+        pb=vm((16, D), F32),
+        ub=vm((16, ff), F32),
+        bq=vm((LAYERS, 8, PACK), F32),
+        xf=vm((LAYERS, rows, D), BF),
+        qkv=vm((LAYERS, rows, PACK), BF),
+        prob=vm((LAYERS, LOCAL_HEADS, rows, rows), BF),
+        mix=vm((LAYERS, rows, 256), F32),
+        mixl=vm((LAYERS, rows, 256), BF),
+        xh1=vm((LAYERS, half, D), F32),
+        iv1=vm((LAYERS, half, 128), F32),
+        nl=vm((LAYERS, rows, D), BF),
+        gp=vm((LAYERS, rows, ff), F32),
+        act=vm((LAYERS, rows, ff), BF),
+        xh2=vm((LAYERS, half, D), F32),
+        iv2=vm((LAYERS, half, 128), F32),
+        stream=vm((half, D), F32),
+        normed=vm((half, D), F32),
+        ct=vm((half, D), BF),
+        ownp=vm((half, D), F32),
+        sibs=vm((2, half, D), BF),
+        sibr=vm((2, half, D), BF),
+        xs=vm((2, half, D), BF),
+        xr=vm((2, half, D), BF),
+        dl=vm((rows, D), BF),
+        db=vm((rows, D), BF),
+        du=vm((rows, ff), BF),
+        dq=vm((rows, PACK), BF),
+        dm=vm((rows, 256), BF),
+        ds=vm((rows, rows), BF),
+        back=vm((2, half, D), BF),
+        land=vm((2, 2, rows // (2 * nz), D), BF),
+        gq=vm((LAYERS, nz, 2, ny, two, PACK), BF),
+        gu=vm((LAYERS, nz, 2, ny, two, ff), BF),
+        gd=vm((LAYERS, nz, ny, f_rows, D), BF),
+        go=vm((LAYERS, nz, ny, 32, D), BF),
+        ryq=vm((LAYERS, nz, 2, two, PACK), BF),
+        ryu=vm((LAYERS, nz, 2, two, ff), BF),
+        ryd=vm((LAYERS, nz, f_rows, D), BF),
+        ryo=vm((LAYERS, nz, 32, D), BF),
+        rzq=vm((LAYERS, 2, nz - 1, 2, two, PACK), BF),
+        rzu=vm((LAYERS, 2, nz - 1, 2, two, ff), BF),
+        rzd=vm((LAYERS, 2, nz - 1, f_rows, D), BF),
+        rzo=vm((LAYERS, 2, nz - 1, 32, D), BF),
+        fq=vm((LAYERS, 2, two, PACK), F32),
+        fu=vm((LAYERS, 2, two, ff), F32),
+        fo=vm((LAYERS, d_rows, D), F32),
+        oq=vm((LAYERS, MEMBERS, d_rows, PACK), F32),
+        ou=vm((LAYERS, MEMBERS, d_rows, ff), F32),
+        oo=vm((LAYERS, d_rows, D), F32),
+        sg=vm((LAYERS, 8, D), F32),
+        sgy=vm((LAYERS, 8, D), F32),
+        sgt=vm((LAYERS, 8, D), F32),
+        sgz=vm((LAYERS, nz, 8, D), F32),
+        sga=vm((LAYERS, MEMBERS, 8, D), F32),
+        stage_s=dma((3, 3)),
+        stage_r=dma((3, 3)),
+        perm=dma((2,)),
+        in_s=dma((4, 2)),
+        in_r=dma((4, 2)),
+        inx_s=dma((2, 2)),
+        inx_r=dma((2, 2)),
+        ins_s=dma((1,)),
+        ins_r=dma((1,)),
+        gz_s=dma((8, 2, nz)),
+        gz_r=dma((8, 2, nz)),
+        gy_s=dma((8, nz)),
+        gy_r=dma((8, nz)),
+        sib_s=dma((2, half // PIECE)),
+        sib_r=dma((2, half // PIECE)),
+        x_s=dma((2, half // PIECE)),
+        x_r=dma((2, half // PIECE)),
+        ag_s=dma((2, half // PIECE)),
+        ag_r=dma((2, half // PIECE)),
+        ry_s=dma((8,)),
+        ry_r=dma((8,)),
+        rz_s=dma((8, 2, nz)),
+        rz_r=dma((8, 2, nz)),
+        fin_s=dma((LAYERS, 2, 3)),
+        fin_r=dma((LAYERS, 2, 3)),
+        fino=dma((LAYERS, 2)),
+        sgy_s=dma((LAYERS,)),
+        sgy_r=dma((LAYERS,)),
+        sgz_s=dma((LAYERS, nz)),
+        sgz_r=dma((LAYERS, nz)),
+        sga_s=dma((LAYERS, 3)),
+        sga_r=dma((LAYERS, 3)),
+    )
+
+
+def group_kernel(layout, nz, *refs):
+    inp, q_in, u_in, o_in, d_in, s_in, cot = refs[:7]
+    out, gin, q_out, u_out, o_out, d_out, s_out = refs[7:14]
+    S = types.SimpleNamespace(**dict(zip(layout.keys(), refs[14:])))
+    rows = S.dl.shape[0]
+    half = rows // 2
+    block = inp.shape[1]
+    d_rows = d_in.shape[1] // 4
+    f_rows = d_in.shape[1]
+    two = 2 * d_rows
+    ff = S.du.shape[1]
+    pieces = half // PIECE
+    place = lax.axis_index("ctx")
+    lane_f = lax.axis_index("fsdp")
+    z, x = lax.div(place, 2), lax.rem(place, 2)
+    y, c = lax.div(lane_f, 2), lax.rem(lane_f, 2)
+    m = 2 * x + c
+    d = 4 * place + lane_f
+    devices = 8 * nz
+
+    def dev(z_at, x_at, y_at, c_at):
+        return (2 * z_at + x_at, 2 * y_at + c_at)
+
+    def rcopy(source, target, send, recv, to):
+        return pltpu.make_async_remote_copy(
+            src_ref=source,
+            dst_ref=target,
+            send_sem=send,
+            recv_sem=recv,
+            device_id=to,
+            device_id_type=MESH,
+        )
+
+    barrier = pltpu.get_barrier_semaphore()
+
+    def hail(step, carry):
+        other = lax.rem(d + step, devices)
+        pl.semaphore_signal(
+            barrier, inc=1, device_id=(lax.div(other, 4), lax.rem(other, 4)), device_id_type=MESH
+        )
+        return carry
+
+    lax.fori_loop(1, devices, hail, 0)
+    pl.semaphore_wait(barrier, devices - 1)
+
+    relation = ((x, 1 - c), (1 - x, c), (1 - x, 1 - c))
+    sibling = dev(z, x, y, 1 - c)
+    peer = dev(z, 1 - x, y, c)
+    across = dev(z, x, 1 - y, c)
+
+    def stage_copy(kind, r):
+        x_r, c_r = relation[r]
+        m_r = 2 * x_r + c_r
+        source = (s_in, q_in.at[m_r], u_in.at[m_r])[kind]
+        target = (S.smg.at[z, y, m], S.qs.at[m], S.us.at[m])[kind]
+        return rcopy(source, target, S.stage_s.at[kind, r], S.stage_r.at[kind, r], dev(z, x_r, y, c_r))
+
+    def stage_wait(kind, r):
+        x_r, c_r = relation[r]
+        m_r = 2 * x_r + c_r
+        target = (S.smg.at[z, y, m_r], S.qs.at[m_r], S.us.at[m_r])[kind]
+        rcopy(
+            target, target, S.stage_s.at[kind, r], S.stage_r.at[kind, r], dev(z, x_r, y, c_r)
+        ).wait_recv()
+
+    for kind in (1, 0):
+        for r in (1, 2, 0):
+            stage_copy(kind, r).start()
+
+    def own_block(j):
+        return (2 * c + j == z) & (lax.div(z, 2) == c)
+
+    def scatter_in(which, source, target, position):
+        for j in range(2):
+            copy = rcopy(
+                source.at[j],
+                target.at[pl.ds(position, block)],
+                S.in_s.at[which, j],
+                S.in_r.at[which, lax.rem(z, 2)],
+                dev(2 * c + j, x, y, lax.div(z, 2)),
+            )
+
+            @pl.when(own_block(j))
+            def _():
+                target[pl.ds(position, block), :] = source[j]
+
+            @pl.when(jnp.logical_not(own_block(j)))
+            def _():
+                copy.start()
+
+    def scatter_in_wait(which, source, target, base):
+        for k in range(2):
+
+            @pl.when(2 * c + k != z)
+            def _():
+                spot = target.at[pl.ds(base + 2 * block * k, block)]
+                rcopy(
+                    spot, spot, S.in_s.at[which, 0], S.in_r.at[which, k], peer
+                ).wait_recv()
+
+    def scatter_in_drain(which, source, target):
+        for j in range(2):
+
+            @pl.when(jnp.logical_not(own_block(j)))
+            def _():
+                rcopy(
+                    source.at[j], source.at[j], S.in_s.at[which, j], S.in_r.at[which, 0], peer
+                ).wait_send()
+
+    first = S.xf.at[0]
+    scatter_in(0, inp, first, block * place)
+
+    perm_to = dev(2 * x + y, lax.div(z, 2), c, lax.rem(z, 2))
+    perm_stays = (2 * x + y == z) & (lax.div(z, 2) == x) & (c == y) & (lax.rem(z, 2) == c)
+    perm_copy = rcopy(o_in, S.wog.at[2 * x + y, c], S.perm.at[0], S.perm.at[1], perm_to)
+
+    @pl.when(perm_stays)
+    def _():
+        S.wog[z, y] = o_in[...]
+
+    @pl.when(jnp.logical_not(perm_stays))
+    def _():
+        perm_copy.start()
+
+    for r in (1, 2, 0):
+        stage_copy(2, r).start()
+    S.smg[z, y, m] = s_in[...]
+    S.qs[m] = q_in[m]
+    S.us[m] = u_in[m]
+    for layer in range(LAYERS):
+        S.wd[layer, z, y] = d_in[layer]
+
+    def join(staged, target):
+        for xx in range(2):
+            first_part = staged[2 * xx].astype(F32)
+            second_part = staged[2 * xx + 1].astype(F32)
+            for layer in range(LAYERS):
+                cut = slice(layer * d_rows, (layer + 1) * d_rows)
+                target[layer, z, xx, y] = jnp.concatenate(
+                    [first_part[cut], second_part[cut]], axis=0
+                ).astype(BF)
+
+    def slab(cls, z_at, y_at):
+        return (
+            lambda: S.smg.at[z_at, y_at],
+            lambda: S.wq.at[0, z_at, :, y_at],
+            lambda: S.wog.at[z_at, y_at],
+            lambda: S.wu.at[0, z_at, :, y_at],
+            lambda: S.wd.at[0, z_at, y_at],
+            lambda: S.wq.at[1, z_at, :, y_at],
+            lambda: S.wu.at[1, z_at, :, y_at],
+            lambda: S.wd.at[1, z_at, y_at],
+        )[cls]()
+
+    def z_copy(cls, way, step, z_at):
+        spot = slab(cls, z_at, y)
+        to = dev(z + 1 - 2 * way, x, y, c)
+        return rcopy(spot, spot, S.gz_s.at[cls, way, step], S.gz_r.at[cls, way, step], to)
+
+    def y_copy(cls, z_at):
+        spot = slab(cls, z_at, y)
+        return rcopy(spot, spot, S.gy_s.at[cls, z_at], S.gy_r.at[cls, z_at], across)
+
+    def gather_step(cls, step):
+        @pl.when(z >= step)
+        def _():
+            if step > 0:
+                z_copy(cls, 0, step - 1, z - step).wait_recv()
+            if step < nz - 1:
+
+                @pl.when(z < nz - 1)
+                def _():
+                    z_copy(cls, 0, step, z - step).start()
+
+            y_copy(cls, z - step).start()
+
+        @pl.when(z + step <= nz - 1)
+        def _():
+            if step > 0:
+                z_copy(cls, 1, step - 1, z + step).wait_recv()
+            if step < nz - 1:
+
+                @pl.when(z > 0)
+                def _():
+                    z_copy(cls, 1, step, z + step).start()
+
+            if step > 0:
+                y_copy(cls, z + step).start()
+
+    def gather_wait(cls):
+        def one(t, carry):
+            spot = slab(cls, t, 1 - y)
+            rcopy(spot, spot, S.gy_s.at[cls, t], S.gy_r.at[cls, t], across).wait_recv()
+            return carry
+
+        lax.fori_loop(0, nz, one, 0)
+
+    def gather_drain(cls):
+        for step in range(nz - 1):
+
+            @pl.when((z >= step) & (z < nz - 1))
+            def _():
+                z_copy(cls, 0, step, z - step).wait_send()
+
+            @pl.when((z + step <= nz - 1) & (z > 0))
+            def _():
+                z_copy(cls, 1, step, z + step).wait_send()
+
+        def one(t, carry):
+            y_copy(cls, t).wait_send()
+            return carry
+
+        lax.fori_loop(0, nz, one, 0)
+
+    for r in range(3):
+        stage_wait(1, r)
+    join(S.qs, S.wq)
+    gather_step(1, 0)
+    for r in range(3):
+        stage_wait(0, r)
+    gather_step(0, 0)
+
+    def x_spots(target, base, mine):
+        return [target.at[pl.ds(base + block * (2 * k + mine), block)] for k in range(2)]
+
+    def swap_start(which, target, base):
+        for k, spot in enumerate(x_spots(target, base, x)):
+            rcopy(spot, spot, S.inx_s.at[which, k], S.inx_r.at[which, k], peer).start()
+
+    def swap_wait(which, target, base):
+        for k, spot in enumerate(x_spots(target, base, 1 - x)):
+            rcopy(spot, spot, S.inx_s.at[which, k], S.inx_r.at[which, k], peer).wait_recv()
+        for k, spot in enumerate(x_spots(target, base, x)):
+            rcopy(spot, spot, S.inx_s.at[which, k], S.inx_r.at[which, k], peer).wait_send()
+
+    mine = half * c
+    theirs = half * (1 - c)
+    scatter_in_wait(0, inp, first, mine + block * x)
+    swap_start(0, first, mine)
+    gather_step(1, 1)
+    gather_step(0, 1)
+    for r in range(3):
+        stage_wait(2, r)
+    join(S.us, S.wu)
+    swap_wait(0, first, mine)
+    spot = first.at[pl.ds(mine, half)]
+    rcopy(spot, spot, S.ins_s.at[0], S.ins_r.at[0], sibling).start()
+    S.stream[...] = S.xf[0, pl.ds(mine, half), :].astype(F32)
+    gather_step(1, 2)
+    gather_step(0, 2)
+    gather_step(1, 3)
+    gather_step(0, 3)
+
+    @pl.when(jnp.logical_not(perm_stays))
+    def _():
+        spot = S.wog.at[z, y]
+        rcopy(spot, spot, S.perm.at[0], S.perm.at[1], peer).wait_recv()
+
+    gather_step(2, 0)
+    gather_step(3, 0)
+    gather_step(4, 0)
+    gather_wait(0)
+
+    def small_params():
+        row_shape = (devices * 16, D)
+        lane = lax.broadcasted_iota(jnp.int32, (128, D), 0)
+        col = lax.broadcasted_iota(jnp.int32, (128, D), 1)
+        tile = jnp.where(lax.rem(col, d_rows) == lane, 1.0, 0.0).astype(BF)
+        packs = S.smg[:, :, :, 0:16, :].reshape(devices * 16, 128)
+        spread = dot_nn(packs, tile)
+        owner_row = lax.broadcasted_iota(jnp.int32, row_shape, 0) >> 4
+        zz = owner_row >> 3
+        yy = (owner_row >> 2) & 1
+        xx = (owner_row >> 1) & 1
+        cc = owner_row & 1
+        owner = zz * 8 + xx * 4 + yy * 2 + cc
+        at = lax.div(lax.broadcasted_iota(jnp.int32, row_shape, 1), d_rows)
+        spread = jnp.where(owner == at, spread, 0.0)
+        S.pb[...] = jnp.sum(spread.reshape(devices, 16, D), axis=0)
+        lane = lax.broadcasted_iota(jnp.int32, (128, ff), 0)
+        col = lax.broadcasted_iota(jnp.int32, (128, ff), 1)
+        tile = jnp.where(lax.rem(col, f_rows) == lane, 1.0, 0.0).astype(BF)
+        packs = S.smg[:, :, m, 16:32, :].reshape(2 * nz * 16, 128)
+        spread = dot_nn(packs, tile)
+        row_shape = (2 * nz * 16, ff)
+        owner = lax.broadcasted_iota(jnp.int32, row_shape, 0) >> 4
+        at = lax.div(lax.broadcasted_iota(jnp.int32, row_shape, 1), f_rows)
+        spread = jnp.where(owner == at, spread, 0.0)
+        S.ub[...] = jnp.sum(spread.reshape(2 * nz, 16, ff), axis=0)
+        source = lax.broadcasted_iota(jnp.int32, (D, PACK), 0)
+        target, unused_q, unused_v = packed_lanes((D, PACK), 1)
+        pick = jnp.where(source == target + m * (LOCAL_HEADS * HEAD_DIM), 1.0, 0.0).astype(BF)
+        picked = dot_nn(S.pb[...].astype(BF), pick)
+        unused, is_query, is_value = packed_lanes((1, PACK), 1)
+        for layer in range(LAYERS):
+            base = 8 * layer
+            row = jnp.where(is_query, picked[base : base + 1], 0.0)
+            row = jnp.where(is_value, picked[base + 3 : base + 4], row)
+            S.bq[layer, 0:1, :] = row
+
+    small_params()
+    scatter_in(1, cot, S.ct, block * (2 * lax.rem(z, 2) + x))
+
+    def param(layer, kind):
+        return S.pb[8 * layer + kind : 8 * layer + kind + 1, :]
+
+    def piece_rows(i):
+        return pl.ds(i * PIECE if isinstance(i, int) else pl.multiple_of(i * PIECE, PIECE), PIECE)
+
+    def spread_start(par, i, ref, value):
+        spot_rows = pl.ds(pl.multiple_of(mine + i * PIECE, PIECE), PIECE)
+        ref[spot_rows, :] = value
+        spot = ref.at[spot_rows]
+        rcopy(spot, spot, S.ag_s.at[par, i], S.ag_r.at[par, i], sibling).start()
+
+    def spread_wait(par, ref):
+        def one(i, carry):
+            got = ref.at[pl.ds(pl.multiple_of(theirs + i * PIECE, PIECE), PIECE)]
+            sent = ref.at[pl.ds(pl.multiple_of(mine + i * PIECE, PIECE), PIECE)]
+            rcopy(got, got, S.ag_s.at[par, i], S.ag_r.at[par, i], sibling).wait_recv()
+            rcopy(sent, sent, S.ag_s.at[par, i], S.ag_r.at[par, i], sibling).wait_send()
+            return carry
+
+        lax.fori_loop(0, pieces, one, 0)
+
+    def sib_copy(par, i):
+        at = piece_rows(i)
+        return rcopy(
+            S.sibs.at[par, at], S.sibr.at[par, at], S.sib_s.at[par, i], S.sib_r.at[par, i], sibling
+        )
+
+    def peer_copy(par, i):
+        at = piece_rows(i)
+        return rcopy(S.xs.at[par, at], S.xr.at[par, at], S.x_s.at[par, i], S.x_r.at[par, i], peer)
+
+    def member_sum(par, part, use, filler):
+        S.sibs[par] = part(pl.multiple_of(theirs, half)).astype(BF)
+        for i in range(pieces):
+            sib_copy(par, i).start()
+        S.ownp[...] = part(pl.multiple_of(mine, half))
+
+        def send(i, carry):
+            at = piece_rows(i)
+            sib_copy(par, i).wait_recv()
+            S.xs[par, at, :] = (S.ownp[at, :] + S.sibr[par, at, :].astype(F32)).astype(BF)
+            peer_copy(par, i).start()
+            return carry
+
+        lax.fori_loop(0, pieces, send, 0)
+        filler()
+
+        def take(i, carry):
+            at = piece_rows(i)
+            peer_copy(par, i).wait_recv()
+            use(i, S.xs[par, at, :].astype(F32) + S.xr[par, at, :].astype(F32))
+            return carry
+
+        lax.fori_loop(0, pieces, take, 0)
+
+        def drain(i, carry):
+            sib_copy(par, i).wait_send()
+            peer_copy(par, i).wait_send()
+            return carry
+
+        lax.fori_loop(0, pieces, drain, 0)
+
+    def norm_piece(total, at, layer, gain, shift, scaled_ref, inv_ref):
+        centred = total - jnp.mean(total, axis=1, keepdims=True)
+        inv = lax.rsqrt(jnp.mean(centred * centred, axis=1, keepdims=True) + 1e-12)
+        scaled = centred * inv
+        scaled_ref[layer, at, :] = scaled
+        inv_ref[layer, at, :] = jnp.broadcast_to(inv, (PIECE, 128))
+        return scaled * gain + shift
+
+    def flat(value):
+        return value.reshape(-1, value.shape[-1])
+
+    lane_low = lax.broadcasted_iota(jnp.int32, (1, 128), 1) < HEAD_DIM
+
+    def swap_lanes(value):
+        return pltpu.roll(value.astype(F32), HEAD_DIM, 1).astype(BF)
+
+    def head_parts(layer, h, at):
+        zero = jnp.zeros((), BF)
+        if h < 2:
+            keep = lane_low if h == 0 else jnp.logical_not(lane_low)
+            queries = S.qkv[layer, at, 0:128]
+        else:
+            keep = lane_low
+            queries = S.qkv[layer, at, 384:512]
+        return jnp.where(keep, queries * jnp.asarray(HEAD_DIM**-0.5, BF), zero)
+
+    def head_keys(layer, h):
+        if h < 2:
+            return S.qkv[layer, :, 128:256]
+        return swap_lanes(S.qkv[layer, :, 384:512])
+
+    def head_values(layer, h):
+        return S.qkv[layer, :, 256:384] if h < 2 else S.qkv[layer, :, 512:640]
+
+    def forward(layer, fill_one, fill_two, last):
+        weight = flat(S.wq[layer])
+        for i in range(2):
+            at = slice(i * half, (i + 1) * half)
+            S.qkv[layer, at, :] = (
+                dot_nn(S.xf[layer, at, :], weight) + S.bq[layer, 0:1, :]
+            ).astype(BF)
+
+        def attend(i, carry):
+            at = pl.ds(pl.multiple_of(i * 128, 128), 128)
+            mixes = []
+            for h in range(LOCAL_HEADS):
+                scores = dot_nt(head_parts(layer, h, at), head_keys(layer, h))
+                weights = jnp.exp(scores - jnp.max(scores, axis=1, keepdims=True))
+                weights = (weights * (1.0 / jnp.sum(weights, axis=1, keepdims=True))).astype(BF)
+                S.prob[layer, h, at, :] = weights
+                mixes.append(dot_nn(weights, head_values(layer, h)))
+            left = jnp.where(lane_low, mixes[0], mixes[1])
+            right = jnp.where(lane_low, mixes[2], 0.0)
+            S.mix[layer, at, 0:128] = left
+            S.mix[layer, at, 128:256] = right
+            S.mixl[layer, at, 0:128] = left.astype(BF)
+            S.mixl[layer, at, 128:256] = right.astype(BF)
+            return carry
+
+        lax.fori_loop(0, rows // 128, attend, 0)
+
+    def mixed_part(layer):
+        return lambda start: dot_nn(S.mixl[layer, pl.ds(start, half), :], S.wo[layer])
+
+    def after_attention(layer):
+        def use(i, total):
+            at = piece_rows(i)
+            total = S.stream[at, :] + total + param(layer, 1)
+            normed = norm_piece(
+                total, at, layer, param(layer, 4), param(layer, 6), S.xh1, S.iv1
+            )
+            S.normed[at, :] = normed
+            spread_start(0, i, S.nl.at[layer], normed.astype(BF))
+
+        return use
+
+    def raise_part(layer):
+        def one(i, carry):
+            at = pl.ds(pl.multiple_of(i * 128, 128), 128)
+            upward = dot_nn(S.nl[layer, at, :], flat(S.wu[layer])) + S.ub[layer : layer + 1, :]
+            cdf = 0.5 * (1.0 + lax.erf(upward * (0.5**0.5)))
+            density = jnp.exp(-0.5 * upward * upward) * ((2.0 * jnp.pi) ** -0.5)
+            S.act[layer, at, :] = (upward * cdf).astype(BF)
+            S.gp[layer, at, :] = cdf + upward * density
+            return carry
+
+        lax.fori_loop(0, rows // 128, one, 0)
+
+    def lower_part(layer):
+        return lambda start: dot_nn(S.act[layer, pl.ds(start, half), :], flat(S.wd[layer]))
+
+    def after_lower(layer):
+        def use(i, total):
+            at = piece_rows(i)
+            total = S.normed[at, :] + total + param(layer, 2)
+            result = norm_piece(
+                total, at, layer, param(layer, 5), param(layer, 7), S.xh2, S.iv2
+            )
+            if layer < LAYERS - 1:
+                S.stream[at, :] = result
+                spread_start(1, i, S.xf.at[layer + 1], result.astype(BF))
+            else:
+                S.back[0, at, :] = result.astype(BF)
+
+        return use
+
+    def scatter_out(which, source):
+        for k in range(2):
+            stays = (2 * c + k == z) & (lax.div(z, 2) == c)
+            spot = source.at[pl.ds(pl.multiple_of(block * (2 * k + x), block), block)]
+            slot = lax.rem(z, 2)
+
+            @pl.when(stays)
+            def _():
+                S.land[which, slot] = spot[...]
+
+            @pl.when(jnp.logical_not(stays))
+            def _():
+                rcopy(
+                    spot,
+                    S.land.at[which, slot],
+                    S.in_s.at[2 + which, k],
+                    S.in_r.at[2 + which, slot],
+                    dev(2 * c + k, x, y, lax.div(z, 2)),
+                ).start()
+
+    def scatter_out_wait(which, source, result):
+        for k in range(2):
+            spot = source.at[pl.ds(pl.multiple_of(block * (2 * k + x), block), block)]
+
+            @pl.when(jnp.logical_not((2 * c + k == z) & (lax.div(z, 2) == c)))
+            def _():
+                rcopy(
+                    spot, spot, S.in_s.at[2 + which, k], S.in_r.at[2 + which, 0], peer
+                ).wait_send()
+
+            @pl.when(jnp.logical_not(own_block(k)))
+            def _():
+                landed = S.land.at[which, k]
+                rcopy(
+                    landed, landed, S.in_s.at[2 + which, 0], S.in_r.at[2 + which, k], peer
+                ).wait_recv()
+
+        result[...] = S.land[which]
+
+    def out_weights():
+        gather_wait(2)
+        for layer in range(LAYERS):
+            cut = slice(layer * d_rows, (layer + 1) * d_rows)
+            parts = [S.wog[t, yy].astype(F32)[cut] for t in range(nz) for yy in range(2)]
+            parts.append(jnp.zeros((256 - 2 * nz * d_rows, D), F32))
+            S.wo[layer] = jnp.concatenate(parts, axis=0).astype(BF)
+
+    nothing = lambda: None
+
+    spot = first.at[pl.ds(theirs, half)]
+    rcopy(spot, spot, S.ins_s.at[0], S.ins_r.at[0], sibling).wait_recv()
+    gather_wait(1)
+    gather_step(2, 1)
+    forward(0, nothing, nothing, False)
+    gather_step(2, 2)
+    gather_step(3, 1)
+    gather_step(2, 3)
+    out_weights()
+
+    def fill_a():
+        gather_step(3, 2)
+        gather_step(4, 1)
+        gather_step(5, 0)
+        gather_step(6, 0)
+        gather_step(7, 0)
+        gather_step(3, 3)
+        gather_step(4, 2)
+        scatter_in_wait(1, cot, S.ct, block * x)
+        swap_start(1, S.ct, 0)
+        gather_wait(3)
+
+    member_sum(0, mixed_part(0), after_attention(0), fill_a)
+    spread_wait(0, S.nl.at[0])
+    raise_part(0)
+    gather_step(4, 3)
+    gather_step(5, 1)
+    gather_wait(4)
+
+    def fill_b():
+        gather_step(5, 2)
+        gather_step(6, 1)
+        gather_step(5, 3)
+        gather_step(7, 1)
+
+    member_sum(1, lower_part(0), after_lower(0), fill_b)
+    spread_wait(1, S.xf.at[1])
+    gather_wait(5)
+    forward(1, nothing, nothing, False)
+    gather_step(6, 2)
+
+    def fill_c():
+        gather_step(7, 2)
+        gather_step(6, 3)
+        gather_step(7, 3)
+        gather_wait(6)
+
+    member_sum(0, mixed_part(1), after_attention(1), fill_c)
+    spread_wait(0, S.nl.at[1])
+    raise_part(1)
+    gather_wait(7)
+    swap_wait(1, S.ct, 0)
+    member_sum(1, lower_part(1), after_lower(1), nothing)
+    scatter_out(0, S.back.at[0])
+
+    S.sg[...] = jnp.zeros_like(S.sg)
+
+    def add_row(layer, kind, value):
+        S.sg[layer, kind : kind + 1, :] += jnp.sum(value, axis=0, keepdims=True)
+
+    def norm_back_piece(grad, at, layer, which):
+        scaled = (S.xh1 if which == 0 else S.xh2)[layer, at, :]
+        inv = (S.iv1 if which == 0 else S.iv2)[layer, at, 0:1]
+        add_row(layer, 2 + which, grad * scaled)
+        add_row(layer, 4 + which, grad)
+        weighted = grad * param(layer, 4 + which)
+        back = (
+            weighted
+            - jnp.mean(weighted, axis=1, keepdims=True)
+            - scaled * jnp.mean(weighted * scaled, axis=1, keepdims=True)
+        ) * inv
+        return back
+
+    def lower_back(layer, i, grad):
+        at = piece_rows(i)
+        back = norm_back_piece(grad, at, layer, 1)
+        S.normed[at, :] = back
+        rounded = back.astype(BF)
+        add_row(layer, 1, rounded.astype(F32))
+        spread_start(0, i, S.dl, rounded)
+
+    def first_back(i, carry):
+        lower_back(LAYERS - 1, i, S.ct[piece_rows(i), :].astype(F32))
+        return carry
+
+    lax.fori_loop(0, pieces, first_back, 0)
+
+    def raise_back(layer):
+        def one(i, carry):
+            at = pl.ds(pl.multiple_of(i * 128, 128), 128)
+            back = dot_nt(S.dl[at, :], flat(S.wd[layer])) * S.gp[layer, at, :]
+            rounded = back.astype(BF)
+            S.du[at, :] = rounded
+            add_row(layer, 6, rounded.astype(F32))
+            return carry
+
+        lax.fori_loop(0, rows // 128, one, 0)
+
+    grads = (S.gq, S.gu, S.gd, S.go)
+    from_y = (S.ryq, S.ryu, S.ryd, S.ryo)
+    from_z = (S.rzq, S.rzu, S.rzd, S.rzo)
+
+    def grad_slab(layer, kind, t, y_at):
+        ref = grads[kind]
+        return ref.at[layer, t, :, y_at] if kind < 2 else ref.at[layer, t, y_at]
+
+    def reduce_y_copy(layer, kind):
+        ref = grads[kind]
+        source = ref.at[layer, :, :, 1 - y] if kind < 2 else ref.at[layer, :, 1 - y]
+        target = from_y[kind].at[layer]
+        n = 4 * layer + kind
+        return rcopy(source, target, S.ry_s.at[n], S.ry_r.at[n], across)
+
+    def reduce_z_copy(layer, kind, way, t):
+        source = grad_slab(layer, kind, t, y)
+        target = from_z[kind].at[layer, way, t - way]
+        n = 4 * layer + kind
+        to = dev(z - 1 + 2 * way, x, y, c)
+        return rcopy(source, target, S.rz_s.at[n, way, t], S.rz_r.at[n, way, t], to)
+
+    def slab_add(target, other):
+        if len(target.shape) == 3:
+            for xx in range(2):
+                target[xx] = (target[xx].astype(F32) + other[xx].astype(F32)).astype(BF)
+        else:
+            target[...] = (target[...].astype(F32) + other[...].astype(F32)).astype(BF)
+
+    def reduce_start(layer, kind):
+        reduce_y_copy(layer, kind).start()
+
+    def reduce_wave(layer, kind, wave):
+        if wave == 0:
+            reduce_y_copy(layer, kind).wait_recv()
+
+            def one(t, carry):
+                slab_add(grad_slab(layer, kind, t, y), from_y[kind].at[layer, t])
+                return carry
+
+            lax.fori_loop(0, nz, one, 0)
+
+        @pl.when(z == nz - 1 - wave)
+        def _():
+            for t in range(nz - 1 - wave):
+                if wave > 0:
+                    copy = reduce_z_copy(layer, kind, 0, t)
+                    copy.wait_recv()
+                    slab_add(grad_slab(layer, kind, t, y), from_z[kind].at[layer, 0, t])
+                reduce_z_copy(layer, kind, 0, t).start()
+
+        @pl.when(z == wave)
+        def _():
+            for t in range(nz - 1, wave, -1):
+                if wave > 0:
+                    copy = reduce_z_copy(layer, kind, 1, t)
+                    copy.wait_recv()
+                    slab_add(grad_slab(layer, kind, t, y), from_z[kind].at[layer, 1, t - 1])
+                reduce_z_copy(layer, kind, 1, t).start()
+
+    final = (S.fq, S.fu, d_out, S.fo)
+
+    def reduce_last(layer, kind):
+        if kind == 3:
+            target = S.fo.at[layer]
+            cut = lambda value: value[0:d_rows]
+        else:
+            target = final[kind].at[layer]
+            cut = lambda value: value
+        target[...] = cut(grad_slab(layer, kind, z, y)[...].astype(F32))
+
+        @pl.when(z < nz - 1)
+        def _():
+            reduce_z_copy(layer, kind, 0, z).wait_recv()
+            target[...] += cut(from_z[kind][layer, 0, z].astype(F32))
+
+        @pl.when(z > 0)
+        def _():
+            reduce_z_copy(layer, kind, 1, z).wait_recv()
+            target[...] += cut(from_z[kind][layer, 1, z - 1].astype(F32))
+
+        if kind < 2:
+            result = (S.oq, S.ou)[kind]
+            for r in (1, 2, 0):
+                hand_copy(layer, kind, r).start()
+            for xx in range(2):
+                for cc in range(2):
+
+                    @pl.when((x == xx) & (c == cc))
+                    def _():
+                        result[layer, 2 * xx + cc] = target[xx, cc * d_rows : (cc + 1) * d_rows, :]
+
+        if kind == 3:
+            @pl.when(owner_stays)
+            def _():
+                S.oo[layer] = target[...]
+
+            @pl.when(jnp.logical_not(owner_stays))
+            def _():
+                owner_copy(layer).start()
+
+    def hand_copy(layer, kind, r):
+        x_r, c_r = relation[r]
+        source = (S.fq, S.fu)[kind].at[
+            layer, x_r, pl.ds(pl.multiple_of(c_r * d_rows, 8), d_rows)
+        ]
+        target = (S.oq, S.ou)[kind].at[layer, m]
+        return rcopy(
+            source,
+            target,
+            S.fin_s.at[layer, kind, r],
+            S.fin_r.at[layer, kind, r],
+            dev(z, x_r, y, c_r),
+        )
+
+    owner_to = dev(2 * x + c, lax.div(z, 2), lax.rem(z, 2), y)
+    owner_stays = (2 * x + c == z) & (lax.div(z, 2) == x) & (lax.rem(z, 2) == y) & (y == c)
+
+    def owner_copy(layer):
+        return rcopy(
+            S.fo.at[layer], S.oo.at[layer], S.fino.at[layer, 0], S.fino.at[layer, 1], owner_to
+        )
+
+    def reduce_drain(layer, kind):
+        reduce_y_copy(layer, kind).wait_send()
+        for t in range(nz):
+
+            @pl.when(z > t)
+            def _():
+                reduce_z_copy(layer, kind, 0, t).wait_send()
+
+            @pl.when(z < t)
+            def _():
+                reduce_z_copy(layer, kind, 1, t).wait_send()
+
+        if kind < 2:
+            for r in range(3):
+                copy = hand_copy(layer, kind, r)
+                copy.wait_send()
+                copy.wait_recv()
+        if kind == 3:
+            @pl.when(jnp.logical_not(owner_stays))
+            def _():
+                owner_copy(layer).wait_send()
+                owner_copy(layer).wait_recv()
+
+    def lower_grad(layer):
+        for i in range(2):
+            value = dot_tn(S.act[layer, :, i * (ff // 2) : (i + 1) * (ff // 2)], S.dl[...])
+            S.gd[layer, i * (nz // 2) : (i + 1) * (nz // 2)] = value.astype(BF).reshape(
+                nz // 2, 2, f_rows, D
+            )
+        reduce_start(layer, 2)
+
+    def raise_grad(layer):
+        for i in range(2):
+            value = dot_tn(S.nl[layer, :, i * (D // 2) : (i + 1) * (D // 2)], S.du[...])
+            S.gu[layer, i * (nz // 2) : (i + 1) * (nz // 2)] = value.astype(BF).reshape(
+                nz // 2, 2, 2, two, ff
+            )
+        reduce_start(layer, 1)
+
+    def out_grad(layer):
+        value = dot_tn(S.mixl[layer], S.db[...])
+        empty = jnp.zeros((32 - d_rows, D), F32)
+        for t in range(nz):
+            for yy in range(2):
+                at = (2 * t + yy) * d_rows
+                S.go[layer, t, yy] = jnp.concatenate(
+                    [value[at : at + d_rows], empty], axis=0
+                ).astype(BF)
+        reduce_start(layer, 3)
+
+    def project_grad(layer):
+        for i in range(2):
+            value = dot_tn(S.xf[layer, :, i * (D // 2) : (i + 1) * (D // 2)], S.dq[...])
+            S.gq[layer, i * (nz // 2) : (i + 1) * (nz // 2)] = value.astype(BF).reshape(
+                nz // 2, 2, 2, two, PACK
+            )
+        reduce_start(layer, 0)
+
+    def branch_back(layer):
+        def use(i, total):
+            at = piece_rows(i)
+            back = norm_back_piece(total + S.normed[at, :], at, layer, 0)
+            S.stream[at, :] = back
+            rounded = back.astype(BF)
+            add_row(layer, 0, rounded.astype(F32))
+            spread_start(1, i, S.db, rounded)
+
+        return use
+
+    def attend_back(layer):
+        for i in range(2):
+            at = slice(i * half, (i + 1) * half)
+            S.dm[at, :] = dot_nt(S.db[at, :], S.wo[layer]).astype(BF)
+        scale = HEAD_DIM**-0.5
+        halves = []
+        for h in range(LOCAL_HEADS):
+            keep = jnp.logical_not(lane_low) if h == 1 else lane_low
+            cols = slice(0, 128) if h < 2 else slice(128, 256)
+
+            def one(i, carry):
+                at = pl.ds(pl.multiple_of(i * 128, 128), 128)
+                grad = S.dm[at, cols]
+                grad = jnp.where(keep, grad, jnp.zeros((), BF))
+                delta = jnp.sum(grad.astype(F32) * S.mix[layer, at, cols], axis=1, keepdims=True)
+                grad_weights = dot_nt(grad, head_values(layer, h))
+                grad_scores = S.prob[layer, h, at, :].astype(F32) * (grad_weights - delta)
+                rounded = grad_scores.astype(BF)
+                S.ds[at, :] = rounded
+                result = dot_nn(rounded, head_keys(layer, h)) * scale
+                if h == 0:
+                    S.dq[at, 0:128] = result.astype(BF)
+                elif h == 1:
+                    old = S.dq[at, 0:128]
+                    S.dq[at, 0:128] = jnp.where(lane_low, old, result.astype(BF))
+                else:
+                    S.dq[at, 384:512] = result.astype(BF)
+                return carry
+
+            lax.fori_loop(0, rows // 128, one, 0)
+            every = slice(0, rows)
+            keys_back = dot_tn(S.ds[...], head_parts(layer, h, every)).astype(BF)
+            values_back = dot_tn(S.prob[layer, h], S.dm[:, cols]).astype(BF)
+            if h == 0:
+                S.dq[:, 128:256] = keys_back
+                S.dq[:, 256:384] = values_back
+            elif h == 1:
+                S.dq[:, 128:256] = jnp.where(lane_low, S.dq[:, 128:256], keys_back)
+                S.dq[:, 256:384] = jnp.where(lane_low, S.dq[:, 256:384], values_back)
+            else:
+                old = S.dq[:, 384:512]
+                S.dq[:, 384:512] = jnp.where(lane_low, old, swap_lanes(keys_back))
+                S.dq[:, 512:640] = jnp.where(lane_low, values_back, jnp.zeros((), BF))
+        S.sg[layer, 7:8, 0:PACK] = jnp.sum(S.dq[...].astype(F32), axis=0, keepdims=True)
+
+    def raise_sum(layer):
+        return lambda start: dot_nt(S.du[pl.ds(start, half), :], flat(S.wu[layer]))
+
+    def project_sum(layer):
+        return lambda start: dot_nt(S.dq[pl.ds(start, half), :], flat(S.wq[layer]))
+
+    def next_back(layer):
+        def use(i, total):
+            at = piece_rows(i)
+            grad = total + S.stream[at, :]
+            if layer > 0:
+                lower_back(layer - 1, i, grad)
+            else:
+                S.back[1, at, :] = grad.astype(BF)
+
+        return use
+
+    def small_y(layer):
+        return rcopy(S.sg.at[layer], S.sgy.at[layer], S.sgy_s.at[layer], S.sgy_r.at[layer], across)
+
+    def small_z(layer, k):
+        to = dev(lax.rem(z + k, nz), x, y, c)
+        return rcopy(
+            S.sgt.at[layer], S.sgz.at[layer, k], S.sgz_s.at[layer, k], S.sgz_r.at[layer, k], to
+        )
+
+    def small_member(layer, r):
+        x_r, c_r = relation[r]
+        return rcopy(
+            S.sgt.at[layer],
+            S.sga.at[layer, m],
+            S.sga_s.at[layer, r],
+            S.sga_r.at[layer, r],
+            dev(z, x_r, y, c_r),
+        )
+
+    def small_one(layer):
+        small_y(layer).start()
+
+    def small_two(layer):
+        small_y(layer).wait_recv()
+        S.sgt[layer] = S.sg[layer] + S.sgy[layer]
+        for k in range(1, nz):
+            small_z(layer, k).start()
+
+    def small_three(layer):
+        for k in range(1, nz):
+            small_z(layer, k).wait_recv()
+        for k in range(1, nz):
+            small_z(layer, k).wait_send()
+        total = S.sgt[layer]
+        for k in range(1, nz):
+            total = total + S.sgz[layer, k]
+        S.sgt[layer] = total
+        for r in range(3):
+            small_member(layer, r).start()
+        S.sga[layer, m] = total
+
+    def small_four(layer):
+        for r in range(3):
+            small_member(layer, r).wait_send()
+            small_member(layer, r).wait_recv()
+        small_y(layer).wait_send()
+        lane = lax.broadcasted_iota(jnp.int32, (D, 128), 1)
+        col = lax.broadcasted_iota(jnp.int32, (D, 128), 0)
+        narrow = lane < d_rows
+        pick = jnp.where((col == d_rows * d + lane) & narrow, 1.0, 0.0)
+        both = S.sga[layer, 2 * x] + S.sga[layer, 2 * x + 1]
+        s_out[layer, 0:8, :] = dot_exact(both, pick)
+        dim, is_query, is_value = packed_lanes((D, 128), 0)
+        hit = (dim == d_rows * (d - 8 * z) + lane) & narrow
+        attn = S.sga[layer, z]
+        s_out[layer, 8:16, :] = dot_exact(attn, jnp.where(hit & is_query, 1.0, 0.0))
+        s_out[layer, 16:24, :] = dot_exact(attn, jnp.where(hit & is_value, 1.0, 0.0))
+        pick = jnp.where((col == f_rows * (2 * z + y) + lane) & (lane < f_rows), 1.0, 0.0)
+        s_out[layer, 24:32, :] = dot_exact(S.sga[layer, m], pick)
+
+    spread_wait(0, S.dl)
+    raise_back(1)
+
+    def fill_d():
+        lower_grad(1)
+        raise_grad(1)
+
+    member_sum(0, raise_sum(1), branch_back(1), fill_d)
+    spread_wait(1, S.db)
+    reduce_wave(1, 2, 0)
+    attend_back(1)
+    reduce_wave(1, 1, 0)
+
+    def fill_e():
+        project_grad(1)
+        out_grad(1)
+        reduce_wave(1, 2, 1)
+        reduce_wave(1, 1, 1)
+        reduce_wave(1, 2, 2)
+
+    member_sum(1, project_sum(1), next_back(1), fill_e)
+    spread_wait(0, S.dl)
+    small_one(1)
+    reduce_wave(1, 0, 0)
+    reduce_wave(1, 1, 2)
+    raise_back(0)
+
+    def fill_f():
+        lower_grad(0)
+        raise_grad(0)
+        reduce_last(1, 2)
+        reduce_wave(1, 3, 0)
+        reduce_wave(1, 0, 1)
+        small_two(1)
+        reduce_last(1, 1)
+
+    member_sum(0, raise_sum(0), branch_back(0), fill_f)
+    spread_wait(1, S.db)
+    reduce_wave(1, 3, 1)
+    reduce_wave(1, 0, 2)
+    reduce_wave(0, 2, 0)
+    small_three(1)
+    attend_back(0)
+    reduce_wave(1, 3, 2)
+    reduce_wave(0, 1, 0)
+    reduce_wave(0, 2, 1)
+    project_grad(0)
+
+    def fill_g():
+        out_grad(0)
+        reduce_last(1, 0)
+        reduce_wave(0, 1, 1)
+        small_one(0)
+        reduce_wave(0, 2, 2)
+        reduce_last(1, 3)
+
+    member_sum(1, project_sum(0), next_back(0), fill_g)
+    scatter_out(1, S.back.at[1])
+    reduce_wave(0, 0, 0)
+    reduce_wave(0, 3, 0)
+    reduce_wave(0, 1, 2)
+    small_two(0)
+    reduce_last(0, 2)
+    small_four(1)
+    reduce_wave(0, 0, 1)
+    reduce_wave(0, 3, 1)
+    reduce_last(0, 1)
+    small_three(0)
+    reduce_wave(0, 0, 2)
+    reduce_wave(0, 3, 2)
+    reduce_last(0, 0)
+    reduce_last(0, 3)
+    small_four(0)
+
+    for kind in range(3):
+        for r in range(3):
+            stage_copy(kind, r).wait_send()
+    scatter_in_drain(0, inp, first)
+    scatter_in_drain(1, cot, S.ct)
+
+    @pl.when(jnp.logical_not(perm_stays))
+    def _():
+        perm_copy.wait_send()
+
+    spot = first.at[pl.ds(mine, half)]
+    rcopy(spot, spot, S.ins_s.at[0], S.ins_r.at[0], sibling).wait_send()
+    for cls in range(8):
+        gather_drain(cls)
+    scatter_out_wait(0, S.back.at[0], out)
+    scatter_out_wait(1, S.back.at[1], gin)
+    for layer in range(LAYERS):
+        for kind in range(4):
+            reduce_drain(layer, kind)
+    q_out[...] = S.oq[...]
+    u_out[...] = S.ou[...]
+    o_out[...] = S.oo[...]
+
+
+def grouped(nz, ny):
+    def run(inputs, w_qkv, w_out, w_up, w_down, biases, value_bias, up_bias, gains, shifts, cotangent):
+        seqs, block, unused = inputs.shape
+        d_rows = w_out.shape[1]
+        f_rows = w_down.shape[1]
+        ff = nz * ny * f_rows
+        rows = 2 * nz * block
+        half = rows // 2
+        heads = w_qkv.reshape(LAYERS, 3, d_rows, MEMBERS, LOCAL_HEADS, HEAD_DIM)
+        order = ((0, 0), (0, 1), (1, 0), (1, 1), (2, 0), (2, 1), (0, 2), (1, 2), (2, 2))
+        columns = [heads[:, kind, :, :, head] for kind, head in order]
+        columns.append(jnp.zeros_like(columns[0]))
+        q_in = jnp.concatenate(columns, axis=3).transpose(2, 0, 1, 3)
+        q_in = q_in.reshape(MEMBERS, LAYERS * d_rows, PACK)
+        u_in = w_up.reshape(LAYERS, d_rows, nz, 2, ny, 2, f_rows).transpose(3, 5, 0, 1, 2, 4, 6)
+        u_in = u_in.reshape(MEMBERS, LAYERS * d_rows, ff)
+        o_in = w_out.reshape(LAYERS * d_rows, D)
+        small = jnp.concatenate([biases, value_bias[:, None], gains, shifts], axis=1)
+        small = jnp.pad(small.reshape(LAYERS * 8, d_rows), ((0, 0), (0, 128 - d_rows)))
+        s_in = jnp.concatenate(
+            [small, jnp.pad(up_bias, ((0, 16 - LAYERS), (0, 128 - f_rows)))], axis=0
+        )
+        layout = scratch_layout(nz, ny, rows, half, d_rows, f_rows)
+        vmem = pl.BlockSpec(memory_space=pltpu.VMEM)
+        shapes = (
+            jax.ShapeDtypeStruct(inputs.shape, BF),
+            jax.ShapeDtypeStruct(inputs.shape, BF),
+            jax.ShapeDtypeStruct((LAYERS, MEMBERS, d_rows, PACK), F32),
+            jax.ShapeDtypeStruct((LAYERS, MEMBERS, d_rows, ff), F32),
+            jax.ShapeDtypeStruct((LAYERS, d_rows, D), F32),
+            jax.ShapeDtypeStruct((LAYERS, f_rows, D), F32),
+            jax.ShapeDtypeStruct((LAYERS, 32, 128), F32),
+        )
+        output, grad_inputs, q_out, u_out, o_out, d_out, s_out = pl.pallas_call(
+            functools.partial(group_kernel, layout, nz),
+            out_shape=shapes,
+            in_specs=[vmem] * 7,
+            out_specs=[vmem] * 7,
+            scratch_shapes=list(layout.values()),
+            compiler_params=pltpu.CompilerParams(
+                collective_id=0, has_side_effects=True, vmem_limit_bytes=KERNEL_VMEM
+            ),
+        )(inputs, q_in, u_in, o_in, w_down, s_in, cotangent)
+        parts = q_out.reshape(LAYERS, MEMBERS, d_rows, PACK // HEAD_DIM, HEAD_DIM)
+        picks = [
+            jnp.stack([parts[:, :, :, order.index((kind, head))] for head in range(LOCAL_HEADS)], axis=3)
+            for kind in range(3)
+        ]
+        grad_qkv = jnp.stack(picks, axis=1).transpose(0, 1, 3, 2, 4, 5).reshape(w_qkv.shape)
+        grad_up = u_out.reshape(LAYERS, 2, 2, d_rows, nz, ny, f_rows).transpose(0, 3, 4, 1, 5, 2, 6)
+        narrow = s_out[:, :, :d_rows]
+        grad_biases = jnp.stack([narrow[:, 15], narrow[:, 0], narrow[:, 1]], axis=1)
+        return (
+            output,
+            grad_inputs,
+            grad_qkv,
+            o_out,
+            grad_up.reshape(w_up.shape),
+            d_out,
+            grad_biases,
+            narrow[:, 23],
+            s_out[:, 30, :f_rows],
+            narrow[:, 2:4],
+            narrow[:, 4:6],
+        )
+
+    return run
 
 
 def part_count(row_count):
@@ -430,9 +1680,22 @@
     )
 
 
+def one_group_per_sequence(mesh, seqs):
+    return mesh.shape["fsdp"] == 4 and mesh.shape["ctx"] == seqs
+
+
 def solution(mesh):
+    def run(*arrays):
+        seqs = arrays[0].shape[0]
+        chosen = grouped(mesh.shape["ctx"] // 2, 2) if one_group_per_sequence(mesh, seqs) else body
+        return on_devices(mesh, chosen)(*arrays)
+
+    return run
+
+
+def on_devices(mesh, chosen):
     return jax.shard_map(
-        body,
+        chosen,
         mesh=mesh,
         in_specs=(
             P("fsdp", "ctx", None),

time: 2550 us -> 283 us (0.11)
  waiting for transfers between devices: 1740 us -> 0 us
  blocking collectives: 434 us -> 0 us
  Pallas kernels: 0 us -> 258 us
  matrix products: 127 us -> 0 us
  local copies, waits for them, and re-layouts: 132 us -> 20.6 us
  other arithmetic: 79.7 us -> 3.02 us
    reduce_scatter x12 -> x0, waiting for transfers between devices: 776 us -> none  [the longest x2 328 us: body(): lax.psum_scatter(local_sums[2], 'ctx', scatter_dimension=0, tiled=True)]
    unnamed x46 -> x0, waiting for transfers between devices: 671 us -> none
    all_gather x10 -> x0, blocking collectives: 347 us -> none  [the longest x2 82.9 us: body(): lax.all_gather(shards[4], ('ctx', 'fsdp'), axis=1, tiled=True)]
    all_gather x16 -> x0, waiting for transfers between devices: 297 us -> none  [the longest x2 114 us: body(): lax.all_gather(shards[3], ('ctx', 'fsdp'), axis=0, tiled=True)]
    pallas_call x0 -> x1, Pallas kernels: none -> 258 us  [run(): pl.pallas_call(functools.partial(group_kernel, layout, nz), out_shape=sha...]
    dot_general x36 -> x0, matrix products: 127 us -> none  [the longest x2 16.7 us: forward_layer(): jnp.dot(normed_low, w_raise, preferred_element_type=jnp.float32)]
    unnamed x3 -> x0, blocking collectives: 86.8 us -> none
    unnamed x295 -> x19, local copies, waits for them, and re-layouts: 48.2 us -> 4.84 us
  transfers between devices with their start and end apart: 37 -> 0, of which waited for: 26 -> 0; matrix products, arithmetic and copies ran while one was open for 13% -> 0% of each run, Pallas kernels for 0% -> 0%
where the time goes in v1:
time: 283 us; the launch traced here: 282 us
  Pallas kernels  258 us (91%)
  local copies, waits for them, and re-layouts  20.6 us (7%)
  other arithmetic  3.02 us (1%)
    pallas_call x1, Pallas kernels, run(): pl.pallas_call(functools.partial(group_kernel, layout, nz), out_shape=sha...  258 us

profile of v1, /device:TPU:1, one launch (start us, length us, event | category | flops | bytes accessed | tf_op | source)
XLA Modules:
  0.0 282.5 jit_solution(17141276851669213725)
XLA Ops:
  0.6 0.0 copy-start.2
  0.7 0.7 copy.229
  1.4 0.7 copy.230
  2.1 0.7 pad_maximum_fusion
  2.8 1.3 fusion.2.refs_5_
  4.0 1.4 reshape.54
  5.4 0.2 copy.246
  5.6 1.0 reshape.55.refs_2_
  6.7 0.0 copy-done.2
  6.7 0.4 reshape.52
  7.0 0.9 fusion.5
  8.1 0.2 concatenate.9
  8.3 0.7 copy.227
  9.0 257.9 %shard_map.194 = (bf16[2,64,768]{2,1,0:T(8,128)(2,1)}, bf16[2,64,768]{2,1,0:T(8,128)(2,1)}, f32[2,4,24,640]{3,2,1,0:T(8,128)}, f32[2,4,24,768]{3,2,1,0:T(8,128)}...) custom-call(bf16[2,64,768]{2,1,0:T(8,128)(2,1)} %refs_0_.1, bf16[4,48,640]{2,1,0:T(8,128)(2,1)} %bitcast.48, ...), custom_call_target="tpu_custom_call" | custom-call | tf_op jit(solution)/shard_map/pallas_call | solution.py:1226
  266.9 1.3 slice.96
  268.2 1.3 fusion.7
  269.5 1.4 fusion.6
  270.9 0.6 copy.234
  271.5 2.1 reshape.60
  273.6 0.0 copy-start.1
  273.6 0.6 copy.233
  274.2 1.9 reshape.61
  276.1 0.0 copy-done.1
  276.1 0.3 reshape.58
  276.4 0.2 fusion.4
  276.7 0.2 fusion.3
  276.9 0.2 maximum_bitcast_fusion.1
  277.1 0.2 maximum_bitcast_fusion.3
  277.3 0.2 maximum_bitcast_fusion.2
  277.5 0.4 maximum_bitcast_fusion
  277.9 0.2 copy.232
  278.1 0.0 copy-start.4
  278.2 0.0 copy-start.3
  278.2 0.0 copy-start.5
  278.2 0.0 copy-start
  278.2 1.4 reshape.59
  279.6 0.0 copy-done.4
  279.6 0.7 copy.253
  280.3 0.0 copy-done.3
  280.3 0.7 copy.254
  281.0 0.0 copy-done.5
  281.0 0.7 copy.255
  281.6 0.0 copy-done
  281.7 0.8 copy.256
  (8 shorter events, 0.1 us)
Async XLA Ops:
  0.6 6.0 %copy-start.2 = (bf16[2,3,24,768]{3,2,1,0:T(8,128)(2,1)S(1)}, bf16[2,3,24,768]{3,2,1,0:T(8,128)(2,1)}, u32[]{:S(2)}) copy-start(bf16[2,3,24,768]{3,2,1,0:T(8,128)(2,1)} %param.12) | copy-start | bytes 663556
  273.6 2.5 copy-start.1
  278.1 1.5 copy-start.4
  278.2 2.1 copy-start.3
  278.2 2.8 copy-start.5
  278.2 3.5 %copy-start = (f32[2,96,768]{2,1,0:T(8,128)S(1)}, f32[2,96,768]{2,1,0:T(8,128)}, u32[]{:S(2)}) copy-start(f32[2,96,768]{2,1,0:T(8,128)} %get-tuple-element.190) | copy-start | bytes 1769476
